TPU v7x, 32 devices: a whole 2x2x4 slice. The times are simulated.
32 devices in a mesh: grp: 4 (over z), leaf: 8 (over y, x, core).
Axes of the slice: x: 2, y: 2, z: 4, core: 2. Of those that a mesh axis runs over, the one named last changes fastest.
Arguments:
- matrix: bfloat16 [32768, 512], P(('grp', 'leaf')), may hold values from -6 to 6
- leaf_basis: bfloat16 [32768, 512], P(('grp', 'leaf')), may hold values from -0.1875 to 0.1875
- leaf_tri: bfloat16 [32, 512, 512], P(('grp', 'leaf')), may hold values from -1.5 to 1.5, as said below
- inner_basis: bfloat16 [4, 8, 3, 1024, 512], P('grp', 'leaf'), may hold values from -1 to 1, as said below
- inner_tri: bfloat16 [4, 8, 3, 512, 512], P('grp', 'leaf'), may hold values from -1.5 to 1.5, as said below
- outer_basis: bfloat16 [4, 8, 2, 1024, 512], P('grp', 'leaf'), may hold values from -1 to 1, as said below
- outer_tri: bfloat16 [4, 8, 2, 512, 512], P('grp', 'leaf'), may hold values from -1.5 to 1.5, as said below
Outputs:
- reduced: bfloat16 [512, 512], P(None, ('grp', 'leaf'))
Inputs may be any that keep to these rules, and one draw needn't show every extreme that they name: `leaf_tri`: upper triangular; diagonal entries between 0.5 and 1.5. `inner_basis`: equal for all leaves under the same inner node of level l. `inner_tri`: upper triangular, diagonal entries between 0.5 and 1.5; equal for all leaves under the same inner node of level l. `outer_basis`: equal for all leaves under the same outer node of level m. `outer_tri`: upper triangular, diagonal entries between 0.5 and 1.5; equal for all leaves under the same outer node of level m.
All inputs are finite; a program needn't handle non-finite values.
Results may differ from a plain program's by a relative error of at most 0.0045.
Values sent between devices are 32-bit elements; how exact they have to be, the bound alone decides.
A program may use at most 64 MiB of HBM per device.

v0:
```python
import jax
import jax.numpy as jnp
from jax import lax
from jax.sharding import PartitionSpec as P

contract = (((0,), (0,)), ((), ()))


def partner_2(array, axis, stride):
    return lax.ppermute(array, axis, [(i, i ^ 1 << stride) for i in range(lax.axis_size(axis))])


def leaf_reflect(panel_rows, reflectors, triangle):
    rank_width = triangle.shape[-1]
    projected = lax.dot_general(
        reflectors, panel_rows, contract, preferred_element_type=jnp.float32
    )
    mixing = lax.dot_general(
        triangle.astype(jnp.float32), projected, contract, precision=lax.Precision.HIGHEST
    )
    return panel_rows[:rank_width].astype(jnp.float32) - jnp.dot(
        reflectors[:rank_width].astype(jnp.float32), mixing, precision=lax.Precision.HIGHEST
    )


def node_reflect(panel_rows, reflectors, triangle):
    rank_width = triangle.shape[-1]
    basis = reflectors.astype(jnp.float32)
    projected = lax.dot_general(basis, panel_rows, contract, precision=lax.Precision.HIGHEST)
    mixing = lax.dot_general(
        triangle.astype(jnp.float32), projected, contract, precision=lax.Precision.HIGHEST
    )
    return panel_rows[:rank_width] - jnp.dot(
        basis[:rank_width], mixing, precision=lax.Precision.HIGHEST
    )


def pair_rows(own_rows, partner, parity):
    lower_first = jnp.concatenate([own_rows, partner], axis=0)
    upper_first = jnp.concatenate([partner, own_rows], axis=0)
    return jnp.where(parity == 0, lower_first, upper_first)


def own_block(full, device_pos, device_count):
    block_width = full.shape[1] // device_count
    return lax.dynamic_slice_in_dim(full, device_pos * block_width, block_width, 1)


def per_device(matrix, leaf_basis, leaf_tri, inner_basis, inner_tri, outer_basis, outer_tri):
    summit = leaf_reflect(matrix, leaf_basis, leaf_tri[0])
    inner_levels = lax.axis_size("leaf").bit_length() - 1
    outer_levels = lax.axis_size("grp").bit_length() - 1
    leaf_pos = lax.axis_index("leaf")
    group_pos = lax.axis_index("grp")
    device_count = lax.axis_size("grp") * lax.axis_size("leaf")
    device_pos = group_pos * lax.axis_size("leaf") + leaf_pos
    for height in range(inner_levels):
        partner = partner_2(summit, "leaf", height)
        parity = jnp.right_shift(leaf_pos, height) & 1
        summit = node_reflect(
            pair_rows(summit, partner, parity), inner_basis[0, 0, height], inner_tri[0, 0, height]
        )
    for height in range(outer_levels):
        partner = partner_2(summit, "grp", height)
        parity = jnp.right_shift(group_pos, height) & 1
        summit = node_reflect(
            pair_rows(summit, partner, parity), outer_basis[0, 0, height], outer_tri[0, 0, height]
        )
    return own_block(summit, device_pos, device_count).astype(jnp.bfloat16)


def solution(mesh):
    placed = (
        P(("grp", "leaf"), None),
        P(("grp", "leaf"), None),
        P(("grp", "leaf"), None, None),
        P("grp", "leaf", None, None, None),
        P("grp", "leaf", None, None, None),
        P("grp", "leaf", None, None, None),
        P("grp", "leaf", None, None, None),
    )
    return jax.shard_map(
        per_device, mesh=mesh, in_specs=placed, out_specs=P(None, ("grp", "leaf")), check_vma=False
    )
```

profile of v0, /device:TPU:0, one launch (start us, length us, event | category | flops | bytes accessed | tf_op | source)
XLA Modules:
  0.0 162.6 jit_solution(9716483905359459655)
XLA Ops:
  0.0 0.0 copy-start
  0.0 0.0 slice-start.1
  0.0 2.4 %fusion.53 = f32[512,512]{1,0:T(8,128)S(1)} fusion(bf16[1024,512]{1,0:T(8,128)(2,1)} %param.8, bf16[1024,512]{1,0:T(8,128)(2,1)} %param.7), kind=kOutput, calls=%fused_computation.61 | convolution fusion | flops 536870912 | bytes 3145728 | tf_op jit(solution)/shard_map/dot_general | solution.py:15
  2.4 0.0 slice-done.1
  2.4 0.2 copy.21
  2.6 0.0 copy-done
  2.6 0.0 copy-start.9
  2.6 1.0 fusion.39
  3.6 0.2 copy-done.9
  3.8 1.0 fusion
  4.9 0.5 collective-permute-start
  5.4 0.0 copy-start.2
  5.4 2.3 %collective-permute-done = f32[512,512]{0,1:T(8,128)S(1)} collective-permute-done((f32[512,512]{0,1:T(8,128)S(1)}, f32[512,512]{0,1:T(8,128)S(1)}, u32[]{:S(2)}, u32[]{:S(2)}) %collective-permute-start) | collective-permute-done | bytes 1048608 | tf_op jit(solution)/shard_map/ppermute | solution.py:10
  7.7 0.4 maximum_select_fusion
  8.1 0.0 copy-done.2
  8.1 0.0 copy-start.6
  8.1 1.8 %fusion.9 = f32[512,512]{1,0:T(8,128)S(1)} fusion(f32[1024,512]{0,1:T(8,128)S(1)} %maximum_select_fusion, bf16[1,1,3,1024,512]{4,3,2,1,0:T(8,128)(2,1)S(1)} %copy-done.2), kind=kOutput, calls=%fused_computation.24 | convolution fusion | flops 3221225472 | bytes 4194304 | tf_op jit(solution)/shard_map/dot_general | solution.py:29
  9.9 0.0 copy-done.6
  9.9 1.0 fusion.37
  10.9 1.0 slice_subtract_fusion.3
  11.9 2.9 %collective-permute-start.1 = (f32[512,512]{0,1:T(8,128)S(1)}, f32[512,512]{0,1:T(8,128)}, u32[]{:S(2)}, u32[]{:S(2)}) collective-permute-start(f32[512,512]{0,1:T(8,128)S(1)} %slice_subtract_fusion.3), channel_id=1, source_target_pairs={{0,2},{1,3},{2,0},{3,1},{4,6},{5,7},{6,4},{7,5},{8,10},{9,11},{10,... | collective-permute-start | bytes 3145736 | tf_op jit(solution)/shard_map/ppermute | solution.py:10
  14.8 0.0 copy-start.3
  14.8 23.6 %collective-permute-done.1 = f32[512,512]{0,1:T(8,128)} collective-permute-done((f32[512,512]{0,1:T(8,128)S(1)}, f32[512,512]{0,1:T(8,128)}, u32[]{:S(2)}, u32[]{:S(2)}) %collective-permute-start.1) | collective-permute-done | bytes 1048608 | tf_op jit(solution)/shard_map/ppermute | solution.py:10
  38.4 2.0 %maximum_select_fusion.1 = f32[1024,512]{0,1:T(8,128)S(1)} fusion(f32[512,512]{0,1:T(8,128)} %collective-permute-done.1, f32[512,512]{0,1:T(8,128)S(1)} %slice_subtract_fusion.3, pred[]{:T(512)S(6)} %eq.18), kind=kLoop, calls=%fused_computation.1 | loop fusion | flops 1572864 | bytes 4194305 | tf_op jit(solution)/shard_map/jit(_where)/select_n | solution.py:41
  40.4 0.0 copy-done.3
  40.4 1.8 %fusion.7 = f32[512,512]{1,0:T(8,128)S(1)} fusion(f32[1024,512]{0,1:T(8,128)S(1)} %maximum_select_fusion.1, bf16[1,1,3,1024,512]{4,3,2,1,0:T(8,128)(2,1)S(1)} %copy-done.3), kind=kOutput, calls=%fused_computation.22 | convolution fusion | flops 3221225472 | bytes 4194304 | tf_op jit(solution)/shard_map/dot_general | solution.py:29
  42.3 1.0 fusion.32
  43.3 1.0 slice_subtract_fusion.2
  44.3 1.8 %collective-permute-start.2 = (f32[512,512]{0,1:T(8,128)S(1)}, f32[512,512]{0,1:T(8,128)}, u32[]{:S(2)}, u32[]{:S(2)}) collective-permute-start(f32[512,512]{0,1:T(8,128)S(1)} %slice_subtract_fusion.2), channel_id=1, source_target_pairs={{0,4},{1,5},{2,6},{3,7},{4,0},{5,1},{6,2},{7,3},{8,12},{9,13},{10,... | collective-permute-start | bytes 3145736 | tf_op jit(solution)/shard_map/ppermute | solution.py:10
  46.1 0.0 copy-start.4
  46.1 23.0 %collective-permute-done.2 = f32[512,512]{0,1:T(8,128)} collective-permute-done((f32[512,512]{0,1:T(8,128)S(1)}, f32[512,512]{0,1:T(8,128)}, u32[]{:S(2)}, u32[]{:S(2)}) %collective-permute-start.2) | collective-permute-done | bytes 1048608 | tf_op jit(solution)/shard_map/ppermute | solution.py:10
  69.1 2.0 %maximum_select_fusion.2 = f32[1024,512]{0,1:T(8,128)S(1)} fusion(f32[512,512]{0,1:T(8,128)} %collective-permute-done.2, f32[512,512]{0,1:T(8,128)S(1)} %slice_subtract_fusion.2, pred[]{:T(512)S(6)} %eq.17), kind=kLoop, calls=%fused_computation.2 | loop fusion | flops 1572864 | bytes 4194305 | tf_op jit(solution)/shard_map/jit(_where)/select_n | solution.py:41
  71.1 0.0 copy-done.4
  71.2 2.0 %fusion.5 = f32[512,512]{1,0:T(8,128)S(1)} fusion(f32[1024,512]{0,1:T(8,128)S(1)} %maximum_select_fusion.2, bf16[1,1,3,1024,512]{4,3,2,1,0:T(8,128)(2,1)S(1)} %copy-done.4), kind=kOutput, calls=%fused_computation.20 | convolution fusion | flops 3221225472 | bytes 4194304 | tf_op jit(solution)/shard_map/dot_general | solution.py:29
  73.2 1.0 fusion.27
  74.2 2.0 %slice_subtract_fusion.1 = f32[512,512]{0,1:T(8,128)} fusion(f32[1024,512]{0,1:T(8,128)S(1)} %maximum_select_fusion.2, f32[512,512]{1,0:T(8,128)S(1)} %fusion.27, bf16[1,1,3,1024,512]{4,3,2,1,0:T(8,128)(2,1)S(1)} %copy-done.4), kind=kOutput, calls=%fused_computation.13 | convolution fusion | flops 1610874880 | bytes 3670016 | tf_op jit(solution)/shard_map/dot_general | solution.py:33
  76.2 1.5 collective-permute-start.3
  77.7 0.0 copy-start.5
  77.7 22.6 %collective-permute-done.3 = f32[512,512]{0,1:T(8,128)} collective-permute-done((f32[512,512]{0,1:T(8,128)}, f32[512,512]{0,1:T(8,128)}, u32[]{:S(2)}, u32[]{:S(2)}) %collective-permute-start.3) | collective-permute-done | bytes 1048608 | tf_op jit(solution)/shard_map/ppermute | solution.py:10
  100.2 2.6 %maximum_select_fusion.3 = f32[1024,512]{0,1:T(8,128)S(1)} fusion(f32[512,512]{0,1:T(8,128)} %collective-permute-done.3, f32[512,512]{0,1:T(8,128)} %slice_subtract_fusion.1, pred[]{:T(512)S(6)} %eq.16), kind=kLoop, calls=%fused_computation.3 | loop fusion | flops 1572864 | bytes 4194305 | tf_op jit(solution)/shard_map/jit(_where)/select_n | solution.py:41
  102.9 0.0 copy-done.5
  102.9 0.0 copy-start.7
  102.9 1.8 %fusion.3 = f32[512,512]{1,0:T(8,128)S(1)} fusion(f32[1024,512]{0,1:T(8,128)S(1)} %maximum_select_fusion.3, bf16[1,1,2,1024,512]{4,3,2,1,0:T(8,128)(2,1)S(1)} %copy-done.5), kind=kOutput, calls=%fused_computation.18 | convolution fusion | flops 3221225472 | bytes 4194304 | tf_op jit(solution)/shard_map/dot_general | solution.py:29
  104.7 0.0 copy-done.7
  104.7 1.0 fusion.22
  105.7 2.0 %slice_subtract_fusion = f32[512,512]{0,1:T(8,128)} fusion(f32[1024,512]{0,1:T(8,128)S(1)} %maximum_select_fusion.3, f32[512,512]{1,0:T(8,128)S(1)} %fusion.22, bf16[1,1,2,1024,512]{4,3,2,1,0:T(8,128)(2,1)S(1)} %copy-done.5), kind=kOutput, calls=%fused_computation.12 | convolution fusion | flops 1610874880 | bytes 3670016 | tf_op jit(solution)/shard_map/dot_general | solution.py:33
  107.7 2.2 %collective-permute-start.4 = (f32[512,512]{0,1:T(8,128)}, f32[512,512]{0,1:T(8,128)}, u32[]{:S(2)}, u32[]{:S(2)}) collective-permute-start(f32[512,512]{0,1:T(8,128)} %slice_subtract_fusion), channel_id=1, source_target_pairs={{0,16},{8,24},{16,0},{24,8},{1,17},{9,25},{17,1},{25,9},{2,18},{10... | collective-permute-start | bytes 3145736 | tf_op jit(solution)/shard_map/ppermute | solution.py:10
  110.0 44.3 %collective-permute-done.4 = f32[512,512]{0,1:T(8,128)} collective-permute-done((f32[512,512]{0,1:T(8,128)}, f32[512,512]{0,1:T(8,128)}, u32[]{:S(2)}, u32[]{:S(2)}) %collective-permute-start.4) | collective-permute-done | bytes 1048608 | tf_op jit(solution)/shard_map/ppermute | solution.py:10
  154.3 2.6 %maximum_select_fusion.4 = f32[1024,512]{0,1:T(8,128)S(1)} fusion(f32[512,512]{0,1:T(8,128)} %collective-permute-done.4, f32[512,512]{0,1:T(8,128)} %slice_subtract_fusion, pred[]{:T(512)S(6)} %eq.15), kind=kLoop, calls=%fused_computation.4 | loop fusion | flops 1572864 | bytes 4194305 | tf_op jit(solution)/shard_map/jit(_where)/select_n | solution.py:41
  156.9 0.0 copy-start.1
  156.9 1.8 %fusion.1 = f32[512,512]{1,0:T(8,128)S(1)} fusion(f32[1024,512]{0,1:T(8,128)S(1)} %maximum_select_fusion.4, bf16[1,1,2,1024,512]{4,3,2,1,0:T(8,128)(2,1)S(1)} %copy-done.5), kind=kOutput, calls=%fused_computation.16 | convolution fusion | flops 3221225472 | bytes 4194304 | tf_op jit(solution)/shard_map/dot_general | solution.py:29
  158.7 0.0 copy-done.1
  158.7 0.0 copy-start.8
  158.8 1.2 copy-done.8
  160.0 0.0 slice-start
  160.0 1.0 fusion.17
  161.0 1.0 convolution_bitcast_fusion
  162.0 0.0 slice-done
  162.0 0.6 fusion.52
Async XLA Ops:
  0.0 2.6 %copy-start = (bf16[1,512,512]{2,1,0:T(8,128)(2,1)S(1)}, bf16[1,512,512]{2,1,0:T(8,128)(2,1)}, u32[]{:S(2)}) copy-start(bf16[1,512,512]{2,1,0:T(8,128)(2,1)} %param.9) | copy-start | bytes 1572868
  0.0 2.4 %slice-start.1 = ((bf16[1024,512]{1,0:T(8,128)(2,1)}), bf16[512,512]{1,0:T(8,128)(2,1)S(1)}, s32[]{:S(2)}) async-start(bf16[1024,512]{1,0:T(8,128)(2,1)} %param.7), calls=%async_computation.1 | async-start | bytes 1048576 | tf_op jit(solution)/shard_map/slice | solution.py:21
  2.6 1.2 copy-start.9
  4.9 2.8 %collective-permute-start = (f32[512,512]{0,1:T(8,128)S(1)}, f32[512,512]{0,1:T(8,128)S(1)}, u32[]{:S(2)}, u32[]{:S(2)}) collective-permute-start(f32[512,512]{0,1:T(8,128)S(1)} %fusion), channel_id=1, source_target_pairs={{0,1},{1,0},{2,3},{3,2},{4,5},{5,4},{6,7},{7,6},{8,9},{9,8},{10,11... | collective-permute-start | bytes 3145736 | tf_op jit(solution)/shard_map/ppermute | solution.py:10
  5.4 2.7 %copy-start.2 = (bf16[1,1,3,1024,512]{4,3,2,1,0:T(8,128)(2,1)S(1)}, bf16[1,1,3,1024,512]{4,3,2,1,0:T(8,128)(2,1)}, u32[]{:S(2)}) copy-start(bf16[1,1,3,1024,512]{4,3,2,1,0:T(8,128)(2,1)} %param.10) | copy-start | bytes 9437188
  8.1 1.8 %copy-start.6 = (bf16[1,1,3,512,512]{4,3,2,1,0:T(8,128)(2,1)S(1)}, bf16[1,1,3,512,512]{4,3,2,1,0:T(8,128)(2,1)}, u32[]{:S(2)}) copy-start(bf16[1,1,3,512,512]{4,3,2,1,0:T(8,128)(2,1)} %param.11) | copy-start | bytes 4718596
  11.9 26.5 %collective-permute-start.1 = (f32[512,512]{0,1:T(8,128)S(1)}, f32[512,512]{0,1:T(8,128)}, u32[]{:S(2)}, u32[]{:S(2)}) collective-permute-start(f32[512,512]{0,1:T(8,128)S(1)} %slice_subtract_fusion.3), channel_id=1, source_target_pairs={{0,2},{1,3},{2,0},{3,1},{4,6},{5,7},{6,4},{7,5},{8,10},{9,11},{10,... | collective-permute-start | bytes 3145736 | tf_op jit(solution)/shard_map/ppermute | solution.py:10
  14.8 25.6 %copy-start.3 = (bf16[1,1,3,1024,512]{4,3,2,1,0:T(8,128)(2,1)S(1)}, bf16[1,1,3,1024,512]{4,3,2,1,0:T(8,128)(2,1)}, u32[]{:S(2)}) copy-start(bf16[1,1,3,1024,512]{4,3,2,1,0:T(8,128)(2,1)} %param.10) | copy-start | bytes 9437188
  44.3 24.9 %collective-permute-start.2 = (f32[512,512]{0,1:T(8,128)S(1)}, f32[512,512]{0,1:T(8,128)}, u32[]{:S(2)}, u32[]{:S(2)}) collective-permute-start(f32[512,512]{0,1:T(8,128)S(1)} %slice_subtract_fusion.2), channel_id=1, source_target_pairs={{0,4},{1,5},{2,6},{3,7},{4,0},{5,1},{6,2},{7,3},{8,12},{9,13},{10,... | collective-permute-start | bytes 3145736 | tf_op jit(solution)/shard_map/ppermute | solution.py:10
  46.1 25.0 %copy-start.4 = (bf16[1,1,3,1024,512]{4,3,2,1,0:T(8,128)(2,1)S(1)}, bf16[1,1,3,1024,512]{4,3,2,1,0:T(8,128)(2,1)}, u32[]{:S(2)}) copy-start(bf16[1,1,3,1024,512]{4,3,2,1,0:T(8,128)(2,1)} %param.10) | copy-start | bytes 9437188
  76.2 24.1 %collective-permute-start.3 = (f32[512,512]{0,1:T(8,128)}, f32[512,512]{0,1:T(8,128)}, u32[]{:S(2)}, u32[]{:S(2)}) collective-permute-start(f32[512,512]{0,1:T(8,128)} %slice_subtract_fusion.1), channel_id=1, source_target_pairs={{0,8},{8,0},{16,24},{24,16},{1,9},{9,1},{17,25},{25,17},{2,10},{10... | collective-permute-start | bytes 3145736 | tf_op jit(solution)/shard_map/ppermute | solution.py:10
  77.7 25.2 %copy-start.5 = (bf16[1,1,2,1024,512]{4,3,2,1,0:T(8,128)(2,1)S(1)}, bf16[1,1,2,1024,512]{4,3,2,1,0:T(8,128)(2,1)}, u32[]{:S(2)}) copy-start(bf16[1,1,2,1024,512]{4,3,2,1,0:T(8,128)(2,1)} %param.12) | copy-start | bytes 6291460
  102.9 1.8 %copy-start.7 = (bf16[1,1,2,512,512]{4,3,2,1,0:T(8,128)(2,1)S(1)}, bf16[1,1,2,512,512]{4,3,2,1,0:T(8,128)(2,1)}, u32[]{:S(2)}) copy-start(bf16[1,1,2,512,512]{4,3,2,1,0:T(8,128)(2,1)} %param.13) | copy-start | bytes 3145732
  107.7 46.5 %collective-permute-start.4 = (f32[512,512]{0,1:T(8,128)}, f32[512,512]{0,1:T(8,128)}, u32[]{:S(2)}, u32[]{:S(2)}) collective-permute-start(f32[512,512]{0,1:T(8,128)} %slice_subtract_fusion), channel_id=1, source_target_pairs={{0,16},{8,24},{16,0},{24,8},{1,17},{9,25},{17,1},{25,9},{2,18},{10... | collective-permute-start | bytes 3145736 | tf_op jit(solution)/shard_map/ppermute | solution.py:10
  156.9 1.8 %copy-start.1 = (f32[1024,512]{0,1:T(8,128)}, f32[1024,512]{0,1:T(8,128)S(1)}, u32[]{:S(2)}) copy-start(f32[1024,512]{0,1:T(8,128)S(1)} %maximum_select_fusion.4) | copy-start | bytes 6291460
  158.7 1.2 copy-start.8
  160.0 2.0 %slice-start = ((f32[1024,512]{0,1:T(8,128)}), f32[512,512]{0,1:T(8,128)S(1)}, s32[]{:S(2)}) async-start(f32[1024,512]{0,1:T(8,128)} %copy-done.1), calls=%async_computation | async-start | bytes 2097152 | tf_op jit(solution)/shard_map/slice | solution.py:33
where the time goes:
time: 163 us
  waiting for transfers between devices  116 us (71%)
  matrix products  25.6 us (16%)
  other arithmetic  10.3 us (6%)
  starting transfers between devices  9.03 us (6%)
  local copies, waits for them, and re-layouts  1.67 us (1%)
    ppermute x5, waiting for transfers between devices, partner_2(): lax.ppermute(array, axis, [(i, i ^ 1 << stride) for i in range(lax.axis_s...  116 us
    select_n x5, other arithmetic, pair_rows(): return jnp.where(parity == 0, lower_first, upper_first)  9.72 us
    dot_general x5, matrix products, node_reflect(): lax.dot_general(basis, panel_rows, contract, precision=lax.Precision.HIGH...  9.18 us
    ppermute x5, starting transfers between devices, partner_2(): lax.ppermute(array, axis, [(i, i ^ 1 << stride) for i in range(lax.axis_s...  9.03 us
    dot_general x5, matrix products, node_reflect(): jnp.dot(basis[:rank_width], mixing, precision=lax.Precision.HIGHEST)  7.07 us
    dot_general x5, matrix products, node_reflect(): lax.dot_general(triangle.astype(jnp.float32), projected, contract, precis...  4.97 us
  transfers between devices with their start and end apart: 5, of which 5 were waited for; matrix products, arithmetic and copies ran while one was open for 0% of the time, Pallas kernels for 0%

commit v1 on v0

v1 whole, which is shorter than its diff:
```python
import functools

import jax
import jax.numpy as jnp
from jax import lax
from jax.experimental import pallas as pl
from jax.experimental.pallas import tpu as pltpu
from jax.sharding import PartitionSpec as P

MESH = pl.DeviceIdType.MESH
F32 = jnp.float32
BF16 = jnp.bfloat16


def dot(left, right):
    return jnp.dot(left, right, preferred_element_type=F32)


def dot_nt(left, right):
    return lax.dot_general(left, right, (((1,), (1,)), ((), ())), preferred_element_type=F32)


def twice(values, product, weights):
    count = values.shape[0]
    high = values.astype(BF16)
    low = (values - high.astype(F32)).astype(BF16)
    both = product(jnp.concatenate([high, low], axis=0), weights)
    return both[:count] + both[count:]


def bit_of(index, height):
    return lax.rem(lax.div(index, 2**height), 2)


def flipped(index, mask):
    for height in range(mask.bit_length()):
        if mask >> height & 1:
            index = index + 2**height * (1 - 2 * bit_of(index, height))
    return index


def reversed_bits(index, count):
    return sum((index >> i & 1) << (count - 1 - i) for i in range(count))


def plan(panel, n_leaf, n_grp):
    inner_rows = panel // n_leaf
    return inner_rows, inner_rows // n_grp >= 8


def axis_orders(bits):
    half = (len(bits) + 1) // 2
    return (bits, bits[half:] + bits[:half])


def kernel(n_leaf, n_grp, *refs):
    (matrix, leaf_basis, leaf_tri, inner_basis, inner_tri, outer_basis, outer_tri, out,
     panel_v, leaf_v, leaf_f, node_v, node_f, first, kept, first_in, parts, parts_in,
     last, last_in, load_sem, send_sem, recv_sem) = refs
    panel = matrix.shape[1]
    k = leaf_tri.shape[-1]
    inner, outer = n_leaf.bit_length() - 1, n_grp.bit_length() - 1
    inner_rows, scatter = plan(panel, n_leaf, n_grp)
    leaf, grp = lax.axis_index("leaf"), lax.axis_index("grp")

    barrier = pltpu.get_barrier_semaphore()
    for height in range(inner):
        pl.semaphore_signal(barrier, inc=1, device_id={"leaf": flipped(leaf, 1 << height)}, device_id_type=MESH)
    for mask in range(1, n_grp):
        pl.semaphore_signal(barrier, inc=1, device_id={"grp": flipped(grp, mask)}, device_id_type=MESH)

    pairs = [(matrix, panel_v), (leaf_basis, leaf_v), (leaf_tri.at[0], leaf_f)]
    for height in range(inner):
        pairs.append((inner_basis.at[0, 0, height], node_v.at[height]))
        pairs.append((inner_tri.at[0, 0, height], node_f.at[height]))
    for height in range(outer):
        pairs.append((outer_basis.at[0, 0, height], node_v.at[inner + height]))
        pairs.append((outer_tri.at[0, 0, height], node_f.at[inner + height]))
    loads = [pltpu.make_async_copy(src, dst, load_sem.at[i]) for i, (src, dst) in enumerate(pairs)]
    for load in loads:
        load.start()

    sent = []

    def send(src, dst, device):
        slot = len(sent)
        copy = pltpu.make_async_remote_copy(
            src_ref=src, dst_ref=dst, send_sem=send_sem.at[slot], recv_sem=recv_sem.at[slot],
            device_id=device, device_id_type=MESH)
        copy.start()
        sent.append(copy)
        return copy

    columns = lax.broadcasted_iota(jnp.int32, (1, panel), 1)
    width = panel // (n_leaf * n_grp)
    owner, target = lax.div(columns, width), lax.rem(columns, width)
    for height in range(inner + outer):
        bit = bit_of(owner, height)
        if height < inner or scatter:
            mine = bit_of(leaf, height) if height < inner else bit_of(grp, height - inner)
            target = target + (bit + mine - 2 * bit * mine) * (panel >> (height + 1))
        else:
            target = target + bit * (width << (height - inner))

    half = panel // 2

    def leaf_rows(start):
        rows = lax.broadcasted_iota(jnp.int32, (half, panel), 0) + start
        order = jnp.where(rows == target, 1.0, 0.0).astype(BF16)
        turned = dot_nt(order, panel_v[...]).astype(BF16)
        mixing = twice(dot(turned, leaf_v[...]), dot, leaf_f[...])
        return turned[:, :k].astype(F32) - twice(mixing, dot_nt, leaf_v[:k, :])

    for load in loads[:3]:
        load.wait()
    first[...] = leaf_rows(half)
    pl.semaphore_wait(barrier, inner + n_grp - 1)
    arriving = send(first, first_in, {"leaf": flipped(leaf, 1)})
    kept[...] = leaf_rows(0)

    def load_node(level):
        loads[3 + 2 * level].wait()
        loads[4 + 2 * level].wait()

    def half_basis(level, parity):
        return node_v[level, pl.ds(pl.multiple_of(parity * k, k), k), :]

    load_node(0)
    parity = bit_of(leaf, 0)
    projected = twice(kept[...], dot, half_basis(0, parity))
    arriving.wait_recv()
    projected = projected + twice(first_in[...], dot, half_basis(0, 1 - parity))
    mixing = twice(projected, dot, node_f[0])
    summit = jnp.where(parity == 0, kept[...], first_in[...]) - twice(mixing, dot_nt, node_v[0, :k, :])

    def own_mixing(summit, level, parity):
        projected = twice(summit, dot, half_basis(level, parity))
        return twice(projected, dot, node_f[level]), jnp.where(parity == 0, summit, 0.0)

    for level in range(1, inner - 1):
        load_node(level)
        mixing, top = own_mixing(summit, level, bit_of(leaf, level))
        summit = top - twice(mixing, dot_nt, node_v[level, :k, :])
    level = inner - 1
    load_node(level)
    mixing, top = own_mixing(summit, level, bit_of(leaf, level))

    bits = tuple(range(1, inner))
    orders = axis_orders(bits)
    lanes = k // 2
    left = [list(bits) for _ in orders]
    waiting = [None, None]

    def pick(group, height, side):
        return (slice(None),) * left[group].index(height) + (side,)

    def send_part(group, step):
        height = orders[group][step]
        waiting[group] = send(
            parts[group][step].at[pick(group, height, 1)], parts_in[group][step],
            {"leaf": flipped(leaf, 1 << height)})

    for group in range(2):
        span = slice(group * lanes, (group + 1) * lanes)
        term = top[:, span] - twice(mixing, dot_nt, node_v[level, span, :])
        parts[group][0][...] = term.reshape(parts[group][0].shape)
        send_part(group, 0)
    sums = [None, None]
    for step in range(len(bits)):
        for group in range(2):
            height = orders[group][step]
            waiting[group].wait_recv()
            total = parts[group][step][pick(group, height, 0)] + parts_in[group][step][...]
            left[group].remove(height)
            if step + 1 < len(bits):
                parts[group][step + 1][...] = total
                send_part(group, step + 1)
            else:
                sums[group] = total
    summit = jnp.concatenate(sums, axis=1)

    for height in range(outer):
        load_node(inner + height)
        mixing, top = own_mixing(summit, inner + height, bit_of(grp, height))
        summit = top - twice(mixing, dot_nt, node_v[inner + height, :k, :])
    last[...] = summit.reshape(last.shape)
    coming = []
    for mask in range(1, n_grp):
        piece = reversed_bits(mask, outer) if scatter else 0
        coming.append(send(last.at[piece], last_in.at[mask - 1], {"grp": flipped(grp, mask)}))
    total = last[0]
    for slot, copy in enumerate(coming):
        copy.wait_recv()
        total = total + last_in[slot]
    out[...] = total.astype(out.dtype)
    for copy in sent:
        copy.wait_send()


def per_device(matrix, leaf_basis, leaf_tri, inner_basis, inner_tri, outer_basis, outer_tri):
    n_leaf, n_grp = lax.axis_size("leaf"), lax.axis_size("grp")
    panel, k = matrix.shape[1], leaf_tri.shape[-1]
    inner, outer = n_leaf.bit_length() - 1, n_grp.bit_length() - 1
    inner_rows, scatter = plan(panel, n_leaf, n_grp)
    levels = inner + outer
    rows = inner_rows // n_grp if scatter else inner_rows
    half = panel // 2
    lead = lambda count: (2,) * count + (inner_rows, k // 2)
    parts = [[pltpu.VMEM(lead(inner - 1 - s), F32) for s in range(inner - 1)] for _ in range(2)]
    parts_in = [[pltpu.VMEM(lead(inner - 2 - s), F32) for s in range(inner - 1)] for _ in range(2)]
    copies = 1 + 2 * (inner - 1) + n_grp - 1
    result = pl.pallas_call(
        functools.partial(kernel, n_leaf, n_grp),
        out_shape=jax.ShapeDtypeStruct((rows, k), BF16),
        in_specs=[pl.BlockSpec(memory_space=pl.ANY)] * 7,
        out_specs=pl.BlockSpec(memory_space=pltpu.VMEM),
        scratch_shapes=[
            pltpu.VMEM(matrix.shape, BF16),
            pltpu.VMEM(leaf_basis.shape, BF16),
            pltpu.VMEM(leaf_tri.shape[1:], BF16),
            pltpu.VMEM((levels,) + inner_basis.shape[-2:], BF16),
            pltpu.VMEM((levels,) + inner_tri.shape[-2:], BF16),
            pltpu.VMEM((half, k), F32),
            pltpu.VMEM((half, k), F32),
            pltpu.VMEM((half, k), F32),
            parts,
            parts_in,
            pltpu.VMEM((n_grp if scatter else 1, rows, k), F32),
            pltpu.VMEM((n_grp - 1, rows, k), F32),
            pltpu.SemaphoreType.DMA((3 + 2 * levels,)),
            pltpu.SemaphoreType.DMA((copies,)),
            pltpu.SemaphoreType.DMA((copies,)),
        ],
        compiler_params=pltpu.CompilerParams(
            collective_id=0, has_side_effects=True, vmem_limit_bytes=60 * 2**20),
        cost_estimate=pl.CostEstimate(flops=30 * 2 * k**3, bytes_accessed=10 * 2**20, transcendentals=0),
    )(matrix, leaf_basis, leaf_tri, inner_basis, inner_tri, outer_basis, outer_tri)
    if not scatter:
        width = panel // (n_leaf * n_grp)
        result = lax.dynamic_slice_in_dim(result, lax.axis_index("grp") * width, width, 0)
    return result.T


def solution(mesh):
    placed = (
        P(("grp", "leaf"), None),
        P(("grp", "leaf"), None),
        P(("grp", "leaf"), None, None),
        P("grp", "leaf", None, None, None),
        P("grp", "leaf", None, None, None),
        P("grp", "leaf", None, None, None),
        P("grp", "leaf", None, None, None),
    )
    return jax.shard_map(
        per_device, mesh=mesh, in_specs=placed, out_specs=P(None, ("grp", "leaf")), check_vma=False
    )
```

time: 163 us -> 29.2 us (0.18)
  waiting for transfers between devices: 116 us -> 0 us
  Pallas kernels: 0 us -> 27.6 us
  matrix products: 25.6 us -> 0 us
  other arithmetic: 10.3 us -> 0 us
  starting transfers between devices: 9.03 us -> 0 us
    ppermute x5 -> x0, waiting for transfers between devices: 116 us -> none  [partner_2(): lax.ppermute(array, axis, [(i, i ^ 1 << stride) for i in range(lax.axis_s...]
    pallas_call x0 -> x1, Pallas kernels: none -> 27.6 us  [per_device(): pl.pallas_call(functools.partial(kernel, n_leaf, n_grp), out_shape=jax.Sh...]
    dot_general x18 -> x0, matrix products: 25.6 us -> none  [the longest x5 9.18 us: node_reflect(): lax.dot_general(basis, panel_rows, contract, precision=lax.Precision.HIGH...]
    select_n x5 -> x0, other arithmetic: 9.72 us -> none  [pair_rows(): return jnp.where(parity == 0, lower_first, upper_first)]
    ppermute x5 -> x0, starting transfers between devices: 9.03 us -> none  [partner_2(): lax.ppermute(array, axis, [(i, i ^ 1 << stride) for i in range(lax.axis_s...]
  transfers between devices with their start and end apart: 5 -> 0, of which waited for: 5 -> 0; matrix products, arithmetic and copies ran while one was open for 0% -> 0% of each run, Pallas kernels for 0% -> 0%
where the time goes in v1:
time: 29.2 us; the launch traced here: 28.9 us
  Pallas kernels  27.6 us (95%)
  local copies, waits for them, and re-layouts  1.32 us (5%)
    pallas_call x1, Pallas kernels, per_device(): pl.pallas_call(functools.partial(kernel, n_leaf, n_grp), out_shape=jax.Sh...  27.6 us
    unnamed x1, local copies, waits for them, and re-layouts  1.32 us

profile of v1, /device:TPU:0, one launch (start us, length us, event | category | flops | bytes accessed | tf_op | source)
XLA Modules:
  0.0 28.9 jit_solution(16300804069697139193)
XLA Ops:
  0.0 27.6 %shard_map.73 = bf16[16,512]{1,0:T(8,128)(2,1)} custom-call(bf16[1024,512]{1,0:T(8,128)(2,1)} %refs_0_.1, bf16[1024,512]{1,0:T(8,128)(2,1)} %refs_1_.1, bf16[1,512,512]{2,1,0:T(8,128)(2,1)} %refs_2_.1, bf16[1,1,3,1024,512]{4,3,2,1,0:T(8,128)(2,1)} %refs_3_.1, bf16[1,1,3,512,512]{4,3,2,1,0:T(8,128)(2,1)} %refs_4_.1, bf16[1,1,2,1024,512]{4,3,2,1,0:T(8,128)(2,1)} %refs_5_.1, ...), custom_call_target="tpu_custom_call" | custom-call | flops 8053063680 | bytes 10485760 | tf_op jit(solution)/shard_map/pallas_call | solution.py:212
  27.6 1.3 %copy.9 = bf16[512,16]{0,1:T(8,128)(2,1)} copy(bf16[512,16]{0,1:T(8,128)(2,1)} %bitcast.1) | data formatting | bytes 32768

commit v2 on v1

v2 whole, which is shorter than its diff:
```python
import functools

import jax
import jax.numpy as jnp
from jax import lax
from jax.experimental import pallas as pl
from jax.experimental.pallas import tpu as pltpu
from jax.sharding import PartitionSpec as P

MESH = pl.DeviceIdType.MESH
F32 = jnp.float32
BF16 = jnp.bfloat16
STREAMS = 2


def dot(left, right):
    return jnp.dot(left, right, preferred_element_type=F32)


def dot_nt(left, right):
    return lax.dot_general(left, right, (((1,), (1,)), ((), ())), preferred_element_type=F32)


def twice(values, product, weights):
    count = values.shape[0]
    high = values.astype(BF16).astype(F32)
    both = product(jnp.concatenate([high, values - high], axis=0).astype(BF16), weights)
    return both[:count] + both[count:]


def bit_of(index, height):
    return lax.rem(lax.div(index, 2**height), 2)


def flipped(index, mask):
    for height in range(mask.bit_length()):
        if mask >> height & 1:
            index = index + 2**height * (1 - 2 * bit_of(index, height))
    return index


def reversed_bits(index, count):
    return sum((index >> i & 1) << (count - 1 - i) for i in range(count))


def plan(panel, n_leaf, n_grp):
    inner_rows = panel // n_leaf // STREAMS
    return inner_rows, inner_rows // n_grp >= 8


def axis_orders(bits):
    half = (len(bits) + 1) // 2
    return (bits, bits[half:] + bits[:half])


def kernel(n_leaf, n_grp, *refs):
    (matrix, leaf_basis, leaf_tri, inner_basis, inner_tri, outer_basis, outer_tri, out,
     panel_v, leaf_v, leaf_f, node_v, node_f, first, kept, first_in, parts, parts_in,
     last, last_in, load_sem, send_sem, recv_sem) = refs
    panel = matrix.shape[1]
    k = leaf_tri.shape[-1]
    inner, outer = n_leaf.bit_length() - 1, n_grp.bit_length() - 1
    inner_rows, scatter = plan(panel, n_leaf, n_grp)
    leaf, grp = lax.axis_index("leaf"), lax.axis_index("grp")

    barrier = pltpu.get_barrier_semaphore()
    for height in range(inner):
        pl.semaphore_signal(barrier, inc=1, device_id={"leaf": flipped(leaf, 1 << height)}, device_id_type=MESH)
    for mask in range(1, n_grp):
        pl.semaphore_signal(barrier, inc=1, device_id={"grp": flipped(grp, mask)}, device_id_type=MESH)

    pairs = [(matrix, panel_v), (leaf_basis, leaf_v), (leaf_tri.at[0], leaf_f)]
    for height in range(inner):
        pairs.append((inner_basis.at[0, 0, height], node_v.at[height]))
        pairs.append((inner_tri.at[0, 0, height], node_f.at[height]))
    for height in range(outer):
        pairs.append((outer_basis.at[0, 0, height], node_v.at[inner + height]))
        pairs.append((outer_tri.at[0, 0, height], node_f.at[inner + height]))
    loads = [pltpu.make_async_copy(src, dst, load_sem.at[i]) for i, (src, dst) in enumerate(pairs)]
    for load in loads:
        load.start()

    sent = []

    def send(src, dst, device):
        slot = len(sent)
        copy = pltpu.make_async_remote_copy(
            src_ref=src, dst_ref=dst, send_sem=send_sem.at[slot], recv_sem=recv_sem.at[slot],
            device_id=device, device_id_type=MESH)
        copy.start()
        sent.append(copy)
        return copy

    columns = lax.broadcasted_iota(jnp.int32, (1, panel), 1)
    stream_rows = panel // STREAMS
    width = panel // (n_leaf * n_grp)
    narrow = width // STREAMS
    owner, place = lax.div(columns, width), lax.rem(columns, width)
    target = lax.div(place, narrow) * stream_rows + lax.rem(place, narrow)
    for height in range(inner + outer):
        bit = bit_of(owner, height)
        if height < inner or scatter:
            mine = bit_of(leaf, height) if height < inner else bit_of(grp, height - inner)
            target = target + (bit + mine - 2 * bit * mine) * (stream_rows >> (height + 1))
        else:
            target = target + bit * (narrow << (height - inner))

    half = stream_rows // 2
    streams = range(STREAMS)

    def leaf_rows(stream):
        rows = lax.broadcasted_iota(jnp.int32, (stream_rows, panel), 0) + stream * stream_rows
        order = jnp.where(rows == target, 1.0, 0.0).astype(BF16)
        turned = dot_nt(order, panel_v[...]).astype(BF16)
        mixing = twice(dot(turned, leaf_v[...]), dot, leaf_f[...])
        return turned[:, :k].astype(F32) - twice(mixing, dot_nt, leaf_v[:k, :])

    def load_node(level):
        loads[3 + 2 * level].wait()
        loads[4 + 2 * level].wait()

    def half_basis(level, parity):
        return node_v[level, pl.ds(pl.multiple_of(parity * k, k), k), :]

    for load in loads[:3]:
        load.wait()
    arriving = []
    for stream in streams:
        summit = leaf_rows(stream)
        kept[stream] = summit[:half]
        first[stream] = summit[half:]
        if stream == 0:
            pl.semaphore_wait(barrier, inner + n_grp - 1)
        arriving.append(send(first.at[stream], first_in.at[stream], {"leaf": flipped(leaf, 1)}))

    def own_mixing(summit, level, parity):
        projected = twice(summit, dot, half_basis(level, parity))
        return twice(projected, dot, node_f[level]), jnp.where(parity == 0, summit, 0.0)

    bits = tuple(range(1, inner))
    orders = axis_orders(bits)
    lanes = k // 2
    left = [[list(bits) for _ in orders] for _ in streams]
    waiting = [[None, None] for _ in streams]

    def pick(stream, group, height, side):
        return (slice(None),) * left[stream][group].index(height) + (side,)

    def send_part(stream, group, step):
        height = orders[group][step]
        waiting[stream][group] = send(
            parts[stream][group][step].at[pick(stream, group, height, 1)], parts_in[stream][group][step],
            {"leaf": flipped(leaf, 1 << height)})

    for level in range(inner):
        load_node(level)
    for stream in streams:
        parity = bit_of(leaf, 0)
        projected = twice(kept[stream], dot, half_basis(0, parity))
        arriving[stream].wait_recv()
        projected = projected + twice(first_in[stream], dot, half_basis(0, 1 - parity))
        mixing = twice(projected, dot, node_f[0])
        top = jnp.where(parity == 0, kept[stream], first_in[stream])
        summit = top - twice(mixing, dot_nt, node_v[0, :k, :])
        for level in range(1, inner - 1):
            mixing, top = own_mixing(summit, level, bit_of(leaf, level))
            summit = top - twice(mixing, dot_nt, node_v[level, :k, :])
        level = inner - 1
        mixing, top = own_mixing(summit, level, bit_of(leaf, level))
        for group in range(2):
            span = slice(group * lanes, (group + 1) * lanes)
            term = top[:, span] - twice(mixing, dot_nt, node_v[level, span, :])
            parts[stream][group][0][...] = term.reshape(parts[stream][group][0].shape)
            send_part(stream, group, 0)

    for height in range(outer):
        load_node(inner + height)
    sums = [[None, None] for _ in streams]
    coming = [[] for _ in streams]
    for step in range(len(bits)):
        for stream in streams:
            for group in range(2):
                height = orders[group][step]
                waiting[stream][group].wait_recv()
                total = parts[stream][group][step][pick(stream, group, height, 0)] + parts_in[stream][group][step][...]
                left[stream][group].remove(height)
                if step + 1 < len(bits):
                    parts[stream][group][step + 1][...] = total
                    send_part(stream, group, step + 1)
                else:
                    sums[stream][group] = total
            if step + 1 == len(bits):
                summit = jnp.concatenate(sums[stream], axis=1)
                for height in range(outer):
                    mixing, top = own_mixing(summit, inner + height, bit_of(grp, height))
                    summit = top - twice(mixing, dot_nt, node_v[inner + height, :k, :])
                last[stream] = summit.reshape(last.shape[1:])
                for mask in range(1, n_grp):
                    piece = reversed_bits(mask, outer) if scatter else 0
                    coming[stream].append(send(
                        last.at[stream, piece], last_in.at[stream, mask - 1], {"grp": flipped(grp, mask)}))
    totals = []
    for stream in streams:
        total = last[stream, 0]
        for slot, copy in enumerate(coming[stream]):
            copy.wait_recv()
            total = total + last_in[stream, slot]
        totals.append(total)
    out[...] = jnp.concatenate(totals, axis=0).astype(out.dtype)
    for copy in sent:
        copy.wait_send()


def per_device(matrix, leaf_basis, leaf_tri, inner_basis, inner_tri, outer_basis, outer_tri):
    n_leaf, n_grp = lax.axis_size("leaf"), lax.axis_size("grp")
    panel, k = matrix.shape[1], leaf_tri.shape[-1]
    inner, outer = n_leaf.bit_length() - 1, n_grp.bit_length() - 1
    inner_rows, scatter = plan(panel, n_leaf, n_grp)
    levels = inner + outer
    rows = inner_rows // n_grp if scatter else inner_rows
    half = panel // STREAMS // 2
    lead = lambda count: (2,) * count + (inner_rows, k // 2)
    steps = range(inner - 1)
    parts = [[[pltpu.VMEM(lead(inner - 1 - s), F32) for s in steps] for _ in range(2)] for _ in range(STREAMS)]
    parts_in = [[[pltpu.VMEM(lead(inner - 2 - s), F32) for s in steps] for _ in range(2)] for _ in range(STREAMS)]
    copies = STREAMS * (1 + 2 * (inner - 1) + n_grp - 1)
    result = pl.pallas_call(
        functools.partial(kernel, n_leaf, n_grp),
        out_shape=jax.ShapeDtypeStruct((STREAMS * rows, k), BF16),
        in_specs=[pl.BlockSpec(memory_space=pl.ANY)] * 7,
        out_specs=pl.BlockSpec(memory_space=pltpu.VMEM),
        scratch_shapes=[
            pltpu.VMEM(matrix.shape, BF16),
            pltpu.VMEM(leaf_basis.shape, BF16),
            pltpu.VMEM(leaf_tri.shape[1:], BF16),
            pltpu.VMEM((levels,) + inner_basis.shape[-2:], BF16),
            pltpu.VMEM((levels,) + inner_tri.shape[-2:], BF16),
            pltpu.VMEM((STREAMS, half, k), F32),
            pltpu.VMEM((STREAMS, half, k), F32),
            pltpu.VMEM((STREAMS, half, k), F32),
            parts,
            parts_in,
            pltpu.VMEM((STREAMS, n_grp if scatter else 1, rows, k), F32),
            pltpu.VMEM((STREAMS, n_grp - 1, rows, k), F32),
            pltpu.SemaphoreType.DMA((3 + 2 * levels,)),
            pltpu.SemaphoreType.DMA((copies,)),
            pltpu.SemaphoreType.DMA((copies,)),
        ],
        compiler_params=pltpu.CompilerParams(
            collective_id=0, has_side_effects=True, vmem_limit_bytes=60 * 2**20),
        cost_estimate=pl.CostEstimate(flops=30 * 2 * k**3, bytes_accessed=10 * 2**20, transcendentals=0),
    )(matrix, leaf_basis, leaf_tri, inner_basis, inner_tri, outer_basis, outer_tri)
    if not scatter:
        narrow = panel // (n_leaf * n_grp) // STREAMS
        result = result.reshape(STREAMS, rows, k)
        result = lax.dynamic_slice_in_dim(result, lax.axis_index("grp") * narrow, narrow, 1)
        result = result.reshape(STREAMS * narrow, k)
    return result.T


def solution(mesh):
    placed = (
        P(("grp", "leaf"), None),
        P(("grp", "leaf"), None),
        P(("grp", "leaf"), None, None),
        P("grp", "leaf", None, None, None),
        P("grp", "leaf", None, None, None),
        P("grp", "leaf", None, None, None),
        P("grp", "leaf", None, None, None),
    )
    return jax.shard_map(
        per_device, mesh=mesh, in_specs=placed, out_specs=P(None, ("grp", "leaf")), check_vma=False
    )
```

time: 29.2 us -> 28.5 us (0.976)
  Pallas kernels: 27.6 us -> 26.9 us
    pallas_call x1, Pallas kernels: 27.6 us -> 26.9 us  [per_device(): pl.pallas_call(functools.partial(kernel, n_leaf, n_grp), out_shape=jax.Sh...]
where the time goes in v2:
time: 28.5 us; the launch traced here: 28.2 us
  Pallas kernels  26.9 us (94%)
  local copies, waits for them, and re-layouts  1.32 us (5%)
    pallas_call x1, Pallas kernels, per_device(): pl.pallas_call(functools.partial(kernel, n_leaf, n_grp), out_shape=jax.Sh...  26.9 us
    unnamed x1, local copies, waits for them, and re-layouts  1.32 us

profile of v2, /device:TPU:0, one launch (start us, length us, event | category | flops | bytes accessed | tf_op | source)
XLA Modules:
  0.0 28.2 jit_solution(11818641911146582432)
XLA Ops:
  0.0 26.9 %shard_map.73 = bf16[16,512]{1,0:T(8,128)(2,1)} custom-call(bf16[1024,512]{1,0:T(8,128)(2,1)} %refs_0_.1, bf16[1024,512]{1,0:T(8,128)(2,1)} %refs_1_.1, bf16[1,512,512]{2,1,0:T(8,128)(2,1)} %refs_2_.1, bf16[1,1,3,1024,512]{4,3,2,1,0:T(8,128)(2,1)} %refs_3_.1, bf16[1,1,3,512,512]{4,3,2,1,0:T(8,128)(2,1)} %refs_4_.1, bf16[1,1,2,1024,512]{4,3,2,1,0:T(8,128)(2,1)} %refs_5_.1, ...), custom_call_target="tpu_custom_call" | custom-call | flops 8053063680 | bytes 10485760 | tf_op jit(solution)/shard_map/pallas_call | solution.py:227
  26.9 1.3 %copy.9 = bf16[512,16]{0,1:T(8,128)(2,1)} copy(bf16[512,16]{0,1:T(8,128)(2,1)} %bitcast.1) | data formatting | bytes 32768

commit v3 on v2

--- a/solution.py
+++ b/solution.py
@@ -24,6 +24,8 @@
 def twice(values, product, weights):
     count = values.shape[0]
     high = values.astype(BF16).astype(F32)
+    if count >= 128:
+        return product(high.astype(BF16), weights) + product((values - high).astype(BF16), weights)
     both = product(jnp.concatenate([high, values - high], axis=0).astype(BF16), weights)
     return both[:count] + both[count:]
 
@@ -77,7 +79,7 @@
         pairs.append((outer_basis.at[0, 0, height], node_v.at[inner + height]))
         pairs.append((outer_tri.at[0, 0, height], node_f.at[inner + height]))
     loads = [pltpu.make_async_copy(src, dst, load_sem.at[i]) for i, (src, dst) in enumerate(pairs)]
-    for load in loads:
+    for load in loads[:3]:
         load.start()
 
     sent = []
@@ -124,6 +126,8 @@
 
     for load in loads[:3]:
         load.wait()
+    for load in loads[3:]:
+        load.start()
     arriving = []
     for stream in streams:
         summit = leaf_rows(stream)

time: 28.5 us -> 29.8 us (1.046)
  Pallas kernels: 26.9 us -> 28.2 us
    pallas_call x1, Pallas kernels: 26.9 us -> 28.2 us  [per_device(): pl.pallas_call(functools.partial(kernel, n_leaf, n_grp), out_shape=jax.Sh...]
where the time goes in v3:
time: 29.8 us; the launch traced here: 29.5 us
  Pallas kernels  28.2 us (95%)
  local copies, waits for them, and re-layouts  1.32 us (4%)
    pallas_call x1, Pallas kernels, per_device(): pl.pallas_call(functools.partial(kernel, n_leaf, n_grp), out_shape=jax.Sh...  28.2 us
    unnamed x1, local copies, waits for them, and re-layouts  1.32 us

profile of v3, /device:TPU:0, one launch (start us, length us, event | category | flops | bytes accessed | tf_op | source)
XLA Modules:
  0.0 29.5 jit_solution(18332694527020368872)
XLA Ops:
  0.0 28.2 %shard_map.73 = bf16[16,512]{1,0:T(8,128)(2,1)} custom-call(bf16[1024,512]{1,0:T(8,128)(2,1)} %refs_0_.1, bf16[1024,512]{1,0:T(8,128)(2,1)} %refs_1_.1, bf16[1,512,512]{2,1,0:T(8,128)(2,1)} %refs_2_.1, bf16[1,1,3,1024,512]{4,3,2,1,0:T(8,128)(2,1)} %refs_3_.1, bf16[1,1,3,512,512]{4,3,2,1,0:T(8,128)(2,1)} %refs_4_.1, bf16[1,1,2,1024,512]{4,3,2,1,0:T(8,128)(2,1)} %refs_5_.1, ...), custom_call_target="tpu_custom_call" | custom-call | flops 8053063680 | bytes 10485760 | tf_op jit(solution)/shard_map/pallas_call | solution.py:231
  28.2 1.3 %copy.9 = bf16[512,16]{0,1:T(8,128)(2,1)} copy(bf16[512,16]{0,1:T(8,128)(2,1)} %bitcast.1) | data formatting | bytes 32768

commit v4 on v3

--- a/solution.py
+++ b/solution.py
@@ -24,8 +24,6 @@
 def twice(values, product, weights):
     count = values.shape[0]
     high = values.astype(BF16).astype(F32)
-    if count >= 128:
-        return product(high.astype(BF16), weights) + product((values - high).astype(BF16), weights)
     both = product(jnp.concatenate([high, values - high], axis=0).astype(BF16), weights)
     return both[:count] + both[count:]
 
@@ -57,7 +55,7 @@
 
 def kernel(n_leaf, n_grp, *refs):
     (matrix, leaf_basis, leaf_tri, inner_basis, inner_tri, outer_basis, outer_tri, out,
-     panel_v, leaf_v, leaf_f, node_v, node_f, first, kept, first_in, parts, parts_in,
+     panel_v, leaf_v, leaf_f, node_v, node_f, outer_high, outer_low, first, kept, first_in, parts, parts_in,
      last, last_in, load_sem, send_sem, recv_sem) = refs
     panel = matrix.shape[1]
     k = leaf_tri.shape[-1]
@@ -94,7 +92,8 @@
         return copy
 
     columns = lax.broadcasted_iota(jnp.int32, (1, panel), 1)
-    stream_rows = panel // STREAMS
+    half = panel // 2
+    stream_rows = half // STREAMS
     width = panel // (n_leaf * n_grp)
     narrow = width // STREAMS
     owner, place = lax.div(columns, width), lax.rem(columns, width)
@@ -103,19 +102,10 @@
         bit = bit_of(owner, height)
         if height < inner or scatter:
             mine = bit_of(leaf, height) if height < inner else bit_of(grp, height - inner)
-            target = target + (bit + mine - 2 * bit * mine) * (stream_rows >> (height + 1))
+            target = target + (bit + mine - 2 * bit * mine) * (stream_rows >> height if height else half)
         else:
             target = target + bit * (narrow << (height - inner))
-
-    half = stream_rows // 2
     streams = range(STREAMS)
-
-    def leaf_rows(stream):
-        rows = lax.broadcasted_iota(jnp.int32, (stream_rows, panel), 0) + stream * stream_rows
-        order = jnp.where(rows == target, 1.0, 0.0).astype(BF16)
-        turned = dot_nt(order, panel_v[...]).astype(BF16)
-        mixing = twice(dot(turned, leaf_v[...]), dot, leaf_f[...])
-        return turned[:, :k].astype(F32) - twice(mixing, dot_nt, leaf_v[:k, :])
 
     def load_node(level):
         loads[3 + 2 * level].wait()
@@ -124,18 +114,24 @@
     def half_basis(level, parity):
         return node_v[level, pl.ds(pl.multiple_of(parity * k, k), k), :]
 
-    for load in loads[:3]:
-        load.wait()
+    rows = lax.broadcasted_iota(jnp.int32, (panel, panel), 0)
+    order = jnp.where(rows == target, 1.0, 0.0).astype(BF16)
+    loads[0].wait()
+    turned = dot_nt(order, panel_v[...]).astype(BF16)
+    loads[1].wait()
+    loads[2].wait()
     for load in loads[3:]:
         load.start()
-    arriving = []
-    for stream in streams:
-        summit = leaf_rows(stream)
-        kept[stream] = summit[:half]
-        first[stream] = summit[half:]
-        if stream == 0:
-            pl.semaphore_wait(barrier, inner + n_grp - 1)
-        arriving.append(send(first.at[stream], first_in.at[stream], {"leaf": flipped(leaf, 1)}))
+    projected = dot(turned, leaf_v[...])
+
+    def leaf_summit(span):
+        mixing = twice(projected[span], dot, leaf_f[...])
+        return turned[span, :k].astype(F32) - twice(mixing, dot_nt, leaf_v[:k, :])
+
+    first[...] = leaf_summit(slice(half, panel))
+    pl.semaphore_wait(barrier, inner + n_grp - 1)
+    arriving = send(first, first_in, {"leaf": flipped(leaf, 1)})
+    kept[...] = leaf_summit(slice(0, half))
 
     def own_mixing(summit, level, parity):
         projected = twice(summit, dot, half_basis(level, parity))
@@ -158,31 +154,50 @@
 
     for level in range(inner):
         load_node(level)
-    for stream in streams:
-        parity = bit_of(leaf, 0)
-        projected = twice(kept[stream], dot, half_basis(0, parity))
-        arriving[stream].wait_recv()
-        projected = projected + twice(first_in[stream], dot, half_basis(0, 1 - parity))
-        mixing = twice(projected, dot, node_f[0])
-        top = jnp.where(parity == 0, kept[stream], first_in[stream])
-        summit = top - twice(mixing, dot_nt, node_v[0, :k, :])
-        for level in range(1, inner - 1):
-            mixing, top = own_mixing(summit, level, bit_of(leaf, level))
-            summit = top - twice(mixing, dot_nt, node_v[level, :k, :])
-        level = inner - 1
+    parity = bit_of(leaf, 0)
+    projected = twice(kept[...], dot, half_basis(0, parity))
+    arriving.wait_recv()
+    projected = projected + twice(first_in[...], dot, half_basis(0, 1 - parity))
+    mixing = twice(projected, dot, node_f[0])
+    top = jnp.where(parity == 0, kept[...], first_in[...])
+    summit = top - twice(mixing, dot_nt, node_v[0, :k, :])
+    for level in range(1, inner - 1):
         mixing, top = own_mixing(summit, level, bit_of(leaf, level))
-        for group in range(2):
-            span = slice(group * lanes, (group + 1) * lanes)
-            term = top[:, span] - twice(mixing, dot_nt, node_v[level, span, :])
-            parts[stream][group][0][...] = term.reshape(parts[stream][group][0].shape)
+        summit = top - twice(mixing, dot_nt, node_v[level, :k, :])
+    level = inner - 1
+    mixing, top = own_mixing(summit, level, bit_of(leaf, level))
+    for group in range(2):
+        span = slice(group * lanes, (group + 1) * lanes)
+        term = top[:, span] - twice(mixing, dot_nt, node_v[level, span, :])
+        for stream in streams:
+            part = term[stream * stream_rows:(stream + 1) * stream_rows]
+            parts[stream][group][0][...] = part.reshape(parts[stream][group][0].shape)
             send_part(stream, group, 0)
 
-    for height in range(outer):
-        load_node(inner + height)
+    def outer_term(height):
+        level, parity = inner + height, bit_of(grp, height)
+        load_node(level)
+        rows = lax.broadcasted_iota(jnp.int32, (k, k), 0)
+        lane = lax.broadcasted_iota(jnp.int32, (k, k), 1)
+        joint = dot_nt(node_f[level], node_v[level, :k, :])
+        high = joint.astype(BF16)
+        low = (joint - high.astype(F32)).astype(BF16)
+        basis = half_basis(level, parity)
+        matrix = jnp.where((rows == lane) & (parity == 0), 1.0, 0.0) - (dot(basis, high) + dot(basis, low))
+        high = matrix.astype(BF16)
+        outer_high[height] = high
+        outer_low[height] = (matrix - high.astype(F32)).astype(BF16)
+
+    def apply_outer(summit, height):
+        return twice(summit, dot, outer_high[height]) + dot(summit.astype(BF16), outer_low[height])
+
     sums = [[None, None] for _ in streams]
     coming = [[] for _ in streams]
+    ahead = list(range(outer))
     for step in range(len(bits)):
         for stream in streams:
+            if ahead:
+                outer_term(ahead.pop(0))
             for group in range(2):
                 height = orders[group][step]
                 waiting[stream][group].wait_recv()
@@ -196,8 +211,7 @@
             if step + 1 == len(bits):
                 summit = jnp.concatenate(sums[stream], axis=1)
                 for height in range(outer):
-                    mixing, top = own_mixing(summit, inner + height, bit_of(grp, height))
-                    summit = top - twice(mixing, dot_nt, node_v[inner + height, :k, :])
+                    summit = apply_outer(summit, height)
                 last[stream] = summit.reshape(last.shape[1:])
                 for mask in range(1, n_grp):
                     piece = reversed_bits(mask, outer) if scatter else 0
@@ -222,12 +236,12 @@
     inner_rows, scatter = plan(panel, n_leaf, n_grp)
     levels = inner + outer
     rows = inner_rows // n_grp if scatter else inner_rows
-    half = panel // STREAMS // 2
+    half = panel // 2
     lead = lambda count: (2,) * count + (inner_rows, k // 2)
     steps = range(inner - 1)
     parts = [[[pltpu.VMEM(lead(inner - 1 - s), F32) for s in steps] for _ in range(2)] for _ in range(STREAMS)]
     parts_in = [[[pltpu.VMEM(lead(inner - 2 - s), F32) for s in steps] for _ in range(2)] for _ in range(STREAMS)]
-    copies = STREAMS * (1 + 2 * (inner - 1) + n_grp - 1)
+    copies = 1 + STREAMS * (2 * (inner - 1) + n_grp - 1)
     result = pl.pallas_call(
         functools.partial(kernel, n_leaf, n_grp),
         out_shape=jax.ShapeDtypeStruct((STREAMS * rows, k), BF16),
@@ -239,9 +253,11 @@
             pltpu.VMEM(leaf_tri.shape[1:], BF16),
             pltpu.VMEM((levels,) + inner_basis.shape[-2:], BF16),
             pltpu.VMEM((levels,) + inner_tri.shape[-2:], BF16),
-            pltpu.VMEM((STREAMS, half, k), F32),
-            pltpu.VMEM((STREAMS, half, k), F32),
-            pltpu.VMEM((STREAMS, half, k), F32),
+            pltpu.VMEM((outer, k, k), BF16),
+            pltpu.VMEM((outer, k, k), BF16),
+            pltpu.VMEM((half, k), F32),
+            pltpu.VMEM((half, k), F32),
+            pltpu.VMEM((half, k), F32),
             parts,
             parts_in,
             pltpu.VMEM((STREAMS, n_grp if scatter else 1, rows, k), F32),

time: 29.8 us -> 27.7 us (0.930)
  Pallas kernels: 28.2 us -> 26.2 us
    pallas_call x1, Pallas kernels: 28.2 us -> 26.2 us  [per_device(): pl.pallas_call(functools.partial(kernel, n_leaf, n_grp), out_shape=jax.Sh...]
where the time goes in v4:
time: 27.7 us; the launch traced here: 27.5 us
  Pallas kernels  26.2 us (95%)
  local copies, waits for them, and re-layouts  1.32 us (5%)
    pallas_call x1, Pallas kernels, per_device(): pl.pallas_call(functools.partial(kernel, n_leaf, n_grp), out_shape=jax.Sh...  26.2 us
    unnamed x1, local copies, waits for them, and re-layouts  1.32 us

profile of v4, /device:TPU:0, one launch (start us, length us, event | category | flops | bytes accessed | tf_op | source)
XLA Modules:
  0.0 27.5 jit_solution(5554910746886144656)
XLA Ops:
  0.0 26.2 %shard_map.73 = bf16[16,512]{1,0:T(8,128)(2,1)} custom-call(bf16[1024,512]{1,0:T(8,128)(2,1)} %refs_0_.1, bf16[1024,512]{1,0:T(8,128)(2,1)} %refs_1_.1, bf16[1,512,512]{2,1,0:T(8,128)(2,1)} %refs_2_.1, bf16[1,1,3,1024,512]{4,3,2,1,0:T(8,128)(2,1)} %refs_3_.1, bf16[1,1,3,512,512]{4,3,2,1,0:T(8,128)(2,1)} %refs_4_.1, bf16[1,1,2,1024,512]{4,3,2,1,0:T(8,128)(2,1)} %refs_5_.1, ...), custom_call_target="tpu_custom_call" | custom-call | flops 8053063680 | bytes 10485760 | tf_op jit(solution)/shard_map/pallas_call | solution.py:245
  26.2 1.3 %copy.9 = bf16[512,16]{0,1:T(8,128)(2,1)} copy(bf16[512,16]{0,1:T(8,128)(2,1)} %bitcast.1) | data formatting | bytes 32768

commit v5 on v4

--- a/solution.py
+++ b/solution.py
@@ -21,10 +21,20 @@
     return lax.dot_general(left, right, (((1,), (1,)), ((), ())), preferred_element_type=F32)
 
 
+def dot_upper(left, right):
+    mid = right.shape[0] // 2
+    return jnp.concatenate([dot(left[:, :mid], right[:mid, :mid]), dot(left, right[:, mid:])], axis=1)
+
+
 def twice(values, product, weights):
     count = values.shape[0]
-    high = values.astype(BF16).astype(F32)
-    both = product(jnp.concatenate([high, values - high], axis=0).astype(BF16), weights)
+    high = values.astype(BF16)
+    low = values - high.astype(F32)
+    if count % 16:
+        stacked = jnp.concatenate([high.astype(F32), low], axis=0).astype(BF16)
+    else:
+        stacked = jnp.concatenate([high, low.astype(BF16)], axis=0)
+    both = product(stacked, weights)
     return both[:count] + both[count:]
 
 
@@ -125,7 +135,7 @@
     projected = dot(turned, leaf_v[...])
 
     def leaf_summit(span):
-        mixing = twice(projected[span], dot, leaf_f[...])
+        mixing = twice(projected[span], dot_upper, leaf_f)
         return turned[span, :k].astype(F32) - twice(mixing, dot_nt, leaf_v[:k, :])
 
     first[...] = leaf_summit(slice(half, panel))
@@ -135,7 +145,7 @@
 
     def own_mixing(summit, level, parity):
         projected = twice(summit, dot, half_basis(level, parity))
-        return twice(projected, dot, node_f[level]), jnp.where(parity == 0, summit, 0.0)
+        return twice(projected, dot_upper, node_f.at[level]), jnp.where(parity == 0, summit, 0.0)
 
     bits = tuple(range(1, inner))
     orders = axis_orders(bits)
@@ -158,19 +168,19 @@
     projected = twice(kept[...], dot, half_basis(0, parity))
     arriving.wait_recv()
     projected = projected + twice(first_in[...], dot, half_basis(0, 1 - parity))
-    mixing = twice(projected, dot, node_f[0])
+    mixing = twice(projected, dot_upper, node_f.at[0])
     top = jnp.where(parity == 0, kept[...], first_in[...])
     summit = top - twice(mixing, dot_nt, node_v[0, :k, :])
-    for level in range(1, inner - 1):
-        mixing, top = own_mixing(summit, level, bit_of(leaf, level))
-        summit = top - twice(mixing, dot_nt, node_v[level, :k, :])
-    level = inner - 1
-    mixing, top = own_mixing(summit, level, bit_of(leaf, level))
-    for group in range(2):
-        span = slice(group * lanes, (group + 1) * lanes)
-        term = top[:, span] - twice(mixing, dot_nt, node_v[level, span, :])
-        for stream in streams:
-            part = term[stream * stream_rows:(stream + 1) * stream_rows]
+    for stream in streams:
+        term = summit[stream * stream_rows:(stream + 1) * stream_rows]
+        for level in range(1, inner - 1):
+            mixing, top = own_mixing(term, level, bit_of(leaf, level))
+            term = top - twice(mixing, dot_nt, node_v[level, :k, :])
+        level = inner - 1
+        mixing, top = own_mixing(term, level, bit_of(leaf, level))
+        for group in range(2):
+            span = slice(group * lanes, (group + 1) * lanes)
+            part = top[:, span] - twice(mixing, dot_nt, node_v[level, span, :])
             parts[stream][group][0][...] = part.reshape(parts[stream][group][0].shape)
             send_part(stream, group, 0)
 
@@ -179,7 +189,10 @@
         load_node(level)
         rows = lax.broadcasted_iota(jnp.int32, (k, k), 0)
         lane = lax.broadcasted_iota(jnp.int32, (k, k), 1)
-        joint = dot_nt(node_f[level], node_v[level, :k, :])
+        mid = k // 2
+        joint = jnp.concatenate([
+            dot_nt(node_f[level, :mid, :], node_v[level, :k, :]),
+            dot_nt(node_f[level, mid:, mid:], node_v[level, :k, mid:])], axis=0)
         high = joint.astype(BF16)
         low = (joint - high.astype(F32)).astype(BF16)
         basis = half_basis(level, parity)
@@ -196,8 +209,6 @@
     ahead = list(range(outer))
     for step in range(len(bits)):
         for stream in streams:
-            if ahead:
-                outer_term(ahead.pop(0))
             for group in range(2):
                 height = orders[group][step]
                 waiting[stream][group].wait_recv()
@@ -208,6 +219,8 @@
                     send_part(stream, group, step + 1)
                 else:
                     sums[stream][group] = total
+            if ahead:
+                outer_term(ahead.pop(0))
             if step + 1 == len(bits):
                 summit = jnp.concatenate(sums[stream], axis=1)
                 for height in range(outer):

time: 27.7 us -> 27.2 us (0.982)
  Pallas kernels: 26.2 us -> 25.6 us
    pallas_call x1, Pallas kernels: 26.2 us -> 25.6 us  [per_device(): pl.pallas_call(functools.partial(kernel, n_leaf, n_grp), out_shape=jax.Sh...]
where the time goes in v5:
time: 27.2 us; the launch traced here: 27 us
  Pallas kernels  25.6 us (94%)
  local copies, waits for them, and re-layouts  1.32 us (5%)
    pallas_call x1, Pallas kernels, per_device(): pl.pallas_call(functools.partial(kernel, n_leaf, n_grp), out_shape=jax.Sh...  25.6 us
    unnamed x1, local copies, waits for them, and re-layouts  1.32 us

profile of v5, /device:TPU:0, one launch (start us, length us, event | category | flops | bytes accessed | tf_op | source)
XLA Modules:
  0.0 27.0 jit_solution(3576994021189117112)
XLA Ops:
  0.0 25.6 %shard_map.73 = bf16[16,512]{1,0:T(8,128)(2,1)} custom-call(bf16[1024,512]{1,0:T(8,128)(2,1)} %refs_0_.1, bf16[1024,512]{1,0:T(8,128)(2,1)} %refs_1_.1, bf16[1,512,512]{2,1,0:T(8,128)(2,1)} %refs_2_.1, bf16[1,1,3,1024,512]{4,3,2,1,0:T(8,128)(2,1)} %refs_3_.1, bf16[1,1,3,512,512]{4,3,2,1,0:T(8,128)(2,1)} %refs_4_.1, bf16[1,1,2,1024,512]{4,3,2,1,0:T(8,128)(2,1)} %refs_5_.1, ...), custom_call_target="tpu_custom_call" | custom-call | flops 8053063680 | bytes 10485760 | tf_op jit(solution)/shard_map/pallas_call | solution.py:258
  25.6 1.3 %copy.9 = bf16[512,16]{0,1:T(8,128)(2,1)} copy(bf16[512,16]{0,1:T(8,128)(2,1)} %bitcast.1) | data formatting | bytes 32768

commit v6 on v5

--- a/solution.py
+++ b/solution.py
@@ -21,21 +21,28 @@
     return lax.dot_general(left, right, (((1,), (1,)), ((), ())), preferred_element_type=F32)
 
 
-def dot_upper(left, right):
-    mid = right.shape[0] // 2
-    return jnp.concatenate([dot(left[:, :mid], right[:mid, :mid]), dot(left, right[:, mid:])], axis=1)
-
-
-def twice(values, product, weights):
-    count = values.shape[0]
+def stack(values):
     high = values.astype(BF16)
     low = values - high.astype(F32)
-    if count % 16:
-        stacked = jnp.concatenate([high.astype(F32), low], axis=0).astype(BF16)
-    else:
-        stacked = jnp.concatenate([high, low.astype(BF16)], axis=0)
-    both = product(stacked, weights)
+    if values.shape[0] % 16:
+        return jnp.concatenate([high.astype(F32), low], axis=0).astype(BF16)
+    return jnp.concatenate([high, low.astype(BF16)], axis=0)
+
+
+def fold(both):
+    count = both.shape[0] // 2
     return both[:count] + both[count:]
+
+
+def join(tiles):
+    return jnp.concatenate(tiles, axis=1)
+
+
+def mix(projected, factor):
+    mid = factor.shape[0] // 2
+    low_tile, high_tile = [stack(tile) for tile in projected]
+    first = stack(fold(dot(low_tile, factor[:mid, :mid])))
+    return join([first, stack(fold(dot(join([low_tile, high_tile]), factor[:, mid:])))])
 
 
 def bit_of(index, height):
@@ -121,8 +128,8 @@
         loads[3 + 2 * level].wait()
         loads[4 + 2 * level].wait()
 
-    def half_basis(level, parity):
-        return node_v[level, pl.ds(pl.multiple_of(parity * k, k), k), :]
+    def half_basis(level, parity, span=slice(None)):
+        return node_v[level, pl.ds(pl.multiple_of(parity * k, k), k), span]
 
     rows = lax.broadcasted_iota(jnp.int32, (panel, panel), 0)
     order = jnp.where(rows == target, 1.0, 0.0).astype(BF16)
@@ -134,22 +141,30 @@
         load.start()
     projected = dot(turned, leaf_v[...])
 
-    def leaf_summit(span):
-        mixing = twice(projected[span], dot_upper, leaf_f)
-        return turned[span, :k].astype(F32) - twice(mixing, dot_nt, leaf_v[:k, :])
-
-    first[...] = leaf_summit(slice(half, panel))
+    mid = k // 2
+    spans = (slice(0, mid), slice(mid, k))
+
+    def leaf_summit(ref, rows):
+        mixing = mix([projected[rows, span] for span in spans], leaf_f)
+        for span in spans:
+            ref[:, span] = turned[rows, span].astype(F32) - fold(dot_nt(mixing, leaf_v[span, :]))
+
+    leaf_summit(first, slice(half, panel))
     pl.semaphore_wait(barrier, inner + n_grp - 1)
     arriving = send(first, first_in, {"leaf": flipped(leaf, 1)})
-    kept[...] = leaf_summit(slice(0, half))
-
-    def own_mixing(summit, level, parity):
-        projected = twice(summit, dot, half_basis(level, parity))
-        return twice(projected, dot_upper, node_f.at[level]), jnp.where(parity == 0, summit, 0.0)
+    leaf_summit(kept, slice(0, half))
+
+    def project(stacked, level, parity):
+        return [fold(dot(stacked, half_basis(level, parity, span))) for span in spans]
+
+    def own_term(tiles, level):
+        parity = bit_of(leaf, level)
+        mixing = mix(project(join([stack(tile) for tile in tiles]), level, parity), node_f.at[level])
+        for tile, span in zip(tiles, spans):
+            yield jnp.where(parity == 0, tile, 0.0) - fold(dot_nt(mixing, node_v[level, span, :]))
 
     bits = tuple(range(1, inner))
     orders = axis_orders(bits)
-    lanes = k // 2
     left = [[list(bits) for _ in orders] for _ in streams]
     waiting = [[None, None] for _ in streams]
 
@@ -165,23 +180,19 @@
     for level in range(inner):
         load_node(level)
     parity = bit_of(leaf, 0)
-    projected = twice(kept[...], dot, half_basis(0, parity))
+    own = project(stack(kept[...]), 0, parity)
     arriving.wait_recv()
-    projected = projected + twice(first_in[...], dot, half_basis(0, 1 - parity))
-    mixing = twice(projected, dot_upper, node_f.at[0])
-    top = jnp.where(parity == 0, kept[...], first_in[...])
-    summit = top - twice(mixing, dot_nt, node_v[0, :k, :])
+    other = project(stack(first_in[...]), 0, 1 - parity)
+    mixing = mix([left_tile + right_tile for left_tile, right_tile in zip(own, other)], node_f.at[0])
+    summit = [
+        jnp.where(parity == 0, kept[:, span], first_in[:, span]) - fold(dot_nt(mixing, node_v[0, span, :]))
+        for span in spans]
     for stream in streams:
-        term = summit[stream * stream_rows:(stream + 1) * stream_rows]
+        tiles = [tile[stream * stream_rows:(stream + 1) * stream_rows] for tile in summit]
         for level in range(1, inner - 1):
-            mixing, top = own_mixing(term, level, bit_of(leaf, level))
-            term = top - twice(mixing, dot_nt, node_v[level, :k, :])
-        level = inner - 1
-        mixing, top = own_mixing(term, level, bit_of(leaf, level))
-        for group in range(2):
-            span = slice(group * lanes, (group + 1) * lanes)
-            part = top[:, span] - twice(mixing, dot_nt, node_v[level, span, :])
-            parts[stream][group][0][...] = part.reshape(parts[stream][group][0].shape)
+            tiles = list(own_term(tiles, level))
+        for group, tile in enumerate(own_term(tiles, inner - 1)):
+            parts[stream][group][0][...] = tile.reshape(parts[stream][group][0].shape)
             send_part(stream, group, 0)
 
     def outer_term(height):
@@ -189,7 +200,6 @@
         load_node(level)
         rows = lax.broadcasted_iota(jnp.int32, (k, k), 0)
         lane = lax.broadcasted_iota(jnp.int32, (k, k), 1)
-        mid = k // 2
         joint = jnp.concatenate([
             dot_nt(node_f[level, :mid, :], node_v[level, :k, :]),
             dot_nt(node_f[level, mid:, mid:], node_v[level, :k, mid:])], axis=0)
@@ -202,7 +212,8 @@
         outer_low[height] = (matrix - high.astype(F32)).astype(BF16)
 
     def apply_outer(summit, height):
-        return twice(summit, dot, outer_high[height]) + dot(summit.astype(BF16), outer_low[height])
+        stacked = stack(summit)
+        return fold(dot(stacked, outer_high[height])) + dot(stacked[:summit.shape[0]], outer_low[height])
 
     sums = [[None, None] for _ in streams]
     coming = [[] for _ in streams]

time: 27.2 us -> 27.2 us (level)
  no operation moved by 1% of the time
where the time goes in v6:
time: 27.2 us; the launch traced here: 27 us
  Pallas kernels  25.6 us (94%)
  local copies, waits for them, and re-layouts  1.32 us (5%)
    pallas_call x1, Pallas kernels, per_device(): pl.pallas_call(functools.partial(kernel, n_leaf, n_grp), out_shape=jax.Sh...  25.6 us
    unnamed x1, local copies, waits for them, and re-layouts  1.32 us

profile of v6, /device:TPU:0, one launch (start us, length us, event | category | flops | bytes accessed | tf_op | source)
XLA Modules:
  0.0 27.0 jit_solution(1854655805402384152)
XLA Ops:
  0.0 25.6 %shard_map.73 = bf16[16,512]{1,0:T(8,128)(2,1)} custom-call(bf16[1024,512]{1,0:T(8,128)(2,1)} %refs_0_.1, bf16[1024,512]{1,0:T(8,128)(2,1)} %refs_1_.1, bf16[1,512,512]{2,1,0:T(8,128)(2,1)} %refs_2_.1, bf16[1,1,3,1024,512]{4,3,2,1,0:T(8,128)(2,1)} %refs_3_.1, bf16[1,1,3,512,512]{4,3,2,1,0:T(8,128)(2,1)} %refs_4_.1, bf16[1,1,2,1024,512]{4,3,2,1,0:T(8,128)(2,1)} %refs_5_.1, ...), custom_call_target="tpu_custom_call" | custom-call | flops 8053063680 | bytes 10485760 | tf_op jit(solution)/shard_map/pallas_call | solution.py:269
  25.6 1.3 %copy.9 = bf16[512,16]{0,1:T(8,128)(2,1)} copy(bf16[512,16]{0,1:T(8,128)(2,1)} %bitcast.1) | data formatting | bytes 32768

commit v7 on v6

--- a/solution.py
+++ b/solution.py
@@ -87,12 +87,10 @@
         pl.semaphore_signal(barrier, inc=1, device_id={"grp": flipped(grp, mask)}, device_id_type=MESH)
 
     pairs = [(matrix, panel_v), (leaf_basis, leaf_v), (leaf_tri.at[0], leaf_f)]
-    for height in range(inner):
-        pairs.append((inner_basis.at[0, 0, height], node_v.at[height]))
-        pairs.append((inner_tri.at[0, 0, height], node_f.at[height]))
-    for height in range(outer):
-        pairs.append((outer_basis.at[0, 0, height], node_v.at[inner + height]))
-        pairs.append((outer_tri.at[0, 0, height], node_f.at[inner + height]))
+    pairs.append((inner_basis.at[0, 0], node_v.at[pl.ds(0, inner)]))
+    pairs.append((inner_tri.at[0, 0], node_f.at[pl.ds(0, inner)]))
+    pairs.append((outer_basis.at[0, 0], node_v.at[pl.ds(inner, outer)]))
+    pairs.append((outer_tri.at[0, 0], node_f.at[pl.ds(inner, outer)]))
     loads = [pltpu.make_async_copy(src, dst, load_sem.at[i]) for i, (src, dst) in enumerate(pairs)]
     for load in loads[:3]:
         load.start()
@@ -124,10 +122,6 @@
             target = target + bit * (narrow << (height - inner))
     streams = range(STREAMS)
 
-    def load_node(level):
-        loads[3 + 2 * level].wait()
-        loads[4 + 2 * level].wait()
-
     def half_basis(level, parity, span=slice(None)):
         return node_v[level, pl.ds(pl.multiple_of(parity * k, k), k), span]
 
@@ -135,24 +129,28 @@
     order = jnp.where(rows == target, 1.0, 0.0).astype(BF16)
     loads[0].wait()
     turned = dot_nt(order, panel_v[...]).astype(BF16)
-    loads[1].wait()
-    loads[2].wait()
     for load in loads[3:]:
         load.start()
+    loads[1].wait()
     projected = dot(turned, leaf_v[...])
+    loads[2].wait()
 
     mid = k // 2
     spans = (slice(0, mid), slice(mid, k))
 
-    def leaf_summit(ref, rows):
+    def leaf_summit(rows):
         mixing = mix([projected[rows, span] for span in spans], leaf_f)
         for span in spans:
-            ref[:, span] = turned[rows, span].astype(F32) - fold(dot_nt(mixing, leaf_v[span, :]))
-
-    leaf_summit(first, slice(half, panel))
-    pl.semaphore_wait(barrier, inner + n_grp - 1)
-    arriving = send(first, first_in, {"leaf": flipped(leaf, 1)})
-    leaf_summit(kept, slice(0, half))
+            yield turned[rows, span].astype(F32) - fold(dot_nt(mixing, leaf_v[span, :]))
+
+    arriving = []
+    for group, tile in enumerate(leaf_summit(slice(half, panel))):
+        first[group] = tile
+        if group == 0:
+            pl.semaphore_wait(barrier, inner + n_grp - 1)
+        arriving.append(send(first.at[group], first_in.at[group], {"leaf": flipped(leaf, 1)}))
+    for group, tile in enumerate(leaf_summit(slice(0, half))):
+        kept[group] = tile
 
     def project(stacked, level, parity):
         return [fold(dot(stacked, half_basis(level, parity, span))) for span in spans]
@@ -177,16 +175,17 @@
             parts[stream][group][step].at[pick(stream, group, height, 1)], parts_in[stream][group][step],
             {"leaf": flipped(leaf, 1 << height)})
 
-    for level in range(inner):
-        load_node(level)
+    loads[3].wait()
+    loads[4].wait()
     parity = bit_of(leaf, 0)
-    own = project(stack(kept[...]), 0, parity)
-    arriving.wait_recv()
-    other = project(stack(first_in[...]), 0, 1 - parity)
+    own = project(join([stack(kept[group]) for group in range(2)]), 0, parity)
+    for copy in arriving:
+        copy.wait_recv()
+    other = project(join([stack(first_in[group]) for group in range(2)]), 0, 1 - parity)
     mixing = mix([left_tile + right_tile for left_tile, right_tile in zip(own, other)], node_f.at[0])
     summit = [
-        jnp.where(parity == 0, kept[:, span], first_in[:, span]) - fold(dot_nt(mixing, node_v[0, span, :]))
-        for span in spans]
+        jnp.where(parity == 0, kept[group], first_in[group]) - fold(dot_nt(mixing, node_v[0, span, :]))
+        for group, span in enumerate(spans)]
     for stream in streams:
         tiles = [tile[stream * stream_rows:(stream + 1) * stream_rows] for tile in summit]
         for level in range(1, inner - 1):
@@ -195,21 +194,23 @@
             parts[stream][group][0][...] = tile.reshape(parts[stream][group][0].shape)
             send_part(stream, group, 0)
 
-    def outer_term(height):
-        level, parity = inner + height, bit_of(grp, height)
-        load_node(level)
+    def halves(values):
+        high = values.astype(BF16)
+        return high, (values - high.astype(F32)).astype(BF16)
+
+    def outer_joint(height):
+        top = node_v.at[inner + height, pl.ds(0, k)]
+        factor = node_f.at[inner + height]
+        return halves(jnp.concatenate([
+            dot_nt(factor[:mid, :], top[...]), dot_nt(factor[mid:, mid:], top[:, mid:])], axis=0))
+
+    def outer_term(height, joint):
+        parity = bit_of(grp, height)
         rows = lax.broadcasted_iota(jnp.int32, (k, k), 0)
         lane = lax.broadcasted_iota(jnp.int32, (k, k), 1)
-        joint = jnp.concatenate([
-            dot_nt(node_f[level, :mid, :], node_v[level, :k, :]),
-            dot_nt(node_f[level, mid:, mid:], node_v[level, :k, mid:])], axis=0)
-        high = joint.astype(BF16)
-        low = (joint - high.astype(F32)).astype(BF16)
-        basis = half_basis(level, parity)
-        matrix = jnp.where((rows == lane) & (parity == 0), 1.0, 0.0) - (dot(basis, high) + dot(basis, low))
-        high = matrix.astype(BF16)
-        outer_high[height] = high
-        outer_low[height] = (matrix - high.astype(F32)).astype(BF16)
+        basis = half_basis(inner + height, parity)
+        matrix = jnp.where((rows == lane) & (parity == 0), 1.0, 0.0) - (dot(basis, joint[0]) + dot(basis, joint[1]))
+        outer_high[height], outer_low[height] = halves(matrix)
 
     def apply_outer(summit, height):
         stacked = stack(summit)
@@ -217,7 +218,9 @@
 
     sums = [[None, None] for _ in streams]
     coming = [[] for _ in streams]
-    ahead = list(range(outer))
+    loads[5].wait()
+    loads[6].wait()
+    joints = []
     for step in range(len(bits)):
         for stream in streams:
             for group in range(2):
@@ -230,8 +233,12 @@
                     send_part(stream, group, step + 1)
                 else:
                     sums[stream][group] = total
-            if ahead:
-                outer_term(ahead.pop(0))
+            if step == 0 and stream == 0:
+                joints = [outer_joint(height) for height in range(outer)]
+                outer_term(0, joints[0])
+            elif step == 0:
+                for height in range(1, outer):
+                    outer_term(height, joints[height])
             if step + 1 == len(bits):
                 summit = jnp.concatenate(sums[stream], axis=1)
                 for height in range(outer):
@@ -265,7 +272,7 @@
     steps = range(inner - 1)
     parts = [[[pltpu.VMEM(lead(inner - 1 - s), F32) for s in steps] for _ in range(2)] for _ in range(STREAMS)]
     parts_in = [[[pltpu.VMEM(lead(inner - 2 - s), F32) for s in steps] for _ in range(2)] for _ in range(STREAMS)]
-    copies = 1 + STREAMS * (2 * (inner - 1) + n_grp - 1)
+    copies = 2 + STREAMS * (2 * (inner - 1) + n_grp - 1)
     result = pl.pallas_call(
         functools.partial(kernel, n_leaf, n_grp),
         out_shape=jax.ShapeDtypeStruct((STREAMS * rows, k), BF16),
@@ -279,14 +286,14 @@
             pltpu.VMEM((levels,) + inner_tri.shape[-2:], BF16),
             pltpu.VMEM((outer, k, k), BF16),
             pltpu.VMEM((outer, k, k), BF16),
-            pltpu.VMEM((half, k), F32),
-            pltpu.VMEM((half, k), F32),
-            pltpu.VMEM((half, k), F32),
+            pltpu.VMEM((2, half, k // 2), F32),
+            pltpu.VMEM((2, half, k // 2), F32),
+            pltpu.VMEM((2, half, k // 2), F32),
             parts,
             parts_in,
             pltpu.VMEM((STREAMS, n_grp if scatter else 1, rows, k), F32),
             pltpu.VMEM((STREAMS, n_grp - 1, rows, k), F32),
-            pltpu.SemaphoreType.DMA((3 + 2 * levels,)),
+            pltpu.SemaphoreType.DMA((7,)),
             pltpu.SemaphoreType.DMA((copies,)),
             pltpu.SemaphoreType.DMA((copies,)),
         ],

time: 27.2 us -> 27.5 us (1.011)
  Pallas kernels: 25.6 us -> 25.9 us
    pallas_call x1, Pallas kernels: 25.6 us -> 25.9 us  [per_device(): pl.pallas_call(functools.partial(kernel, n_leaf, n_grp), out_shape=jax.Sh...]
where the time goes in v7:
time: 27.5 us; the launch traced here: 27.3 us
  Pallas kernels  25.9 us (94%)
  local copies, waits for them, and re-layouts  1.32 us (5%)
    pallas_call x1, Pallas kernels, per_device(): pl.pallas_call(functools.partial(kernel, n_leaf, n_grp), out_shape=jax.Sh...  25.9 us
    unnamed x1, local copies, waits for them, and re-layouts  1.32 us

profile of v7, /device:TPU:0, one launch (start us, length us, event | category | flops | bytes accessed | tf_op | source)
XLA Modules:
  0.0 27.3 jit_solution(16667448396105689268)
XLA Ops:
  0.0 25.9 %shard_map.73 = bf16[16,512]{1,0:T(8,128)(2,1)} custom-call(bf16[1024,512]{1,0:T(8,128)(2,1)} %refs_0_.1, bf16[1024,512]{1,0:T(8,128)(2,1)} %refs_1_.1, bf16[1,512,512]{2,1,0:T(8,128)(2,1)} %refs_2_.1, bf16[1,1,3,1024,512]{4,3,2,1,0:T(8,128)(2,1)} %refs_3_.1, bf16[1,1,3,512,512]{4,3,2,1,0:T(8,128)(2,1)} %refs_4_.1, bf16[1,1,2,1024,512]{4,3,2,1,0:T(8,128)(2,1)} %refs_5_.1, ...), custom_call_target="tpu_custom_call" | custom-call | flops 8053063680 | bytes 10485760 | tf_op jit(solution)/shard_map/pallas_call | solution.py:276
  26.0 1.3 %copy.9 = bf16[512,16]{0,1:T(8,128)(2,1)} copy(bf16[512,16]{0,1:T(8,128)(2,1)} %bitcast.1) | data formatting | bytes 32768

commit v8 on v6

--- a/solution.py
+++ b/solution.py
@@ -94,7 +94,7 @@
         pairs.append((outer_basis.at[0, 0, height], node_v.at[inner + height]))
         pairs.append((outer_tri.at[0, 0, height], node_f.at[inner + height]))
     loads = [pltpu.make_async_copy(src, dst, load_sem.at[i]) for i, (src, dst) in enumerate(pairs)]
-    for load in loads[:3]:
+    for load in loads:
         load.start()
 
     sent = []
@@ -136,10 +136,8 @@
     loads[0].wait()
     turned = dot_nt(order, panel_v[...]).astype(BF16)
     loads[1].wait()
+    projected = dot(turned, leaf_v[...])
     loads[2].wait()
-    for load in loads[3:]:
-        load.start()
-    projected = dot(turned, leaf_v[...])
 
     mid = k // 2
     spans = (slice(0, mid), slice(mid, k))
@@ -177,8 +175,7 @@
             parts[stream][group][step].at[pick(stream, group, height, 1)], parts_in[stream][group][step],
             {"leaf": flipped(leaf, 1 << height)})
 
-    for level in range(inner):
-        load_node(level)
+    load_node(0)
     parity = bit_of(leaf, 0)
     own = project(stack(kept[...]), 0, parity)
     arriving.wait_recv()
@@ -189,8 +186,11 @@
         for span in spans]
     for stream in streams:
         tiles = [tile[stream * stream_rows:(stream + 1) * stream_rows] for tile in summit]
-        for level in range(1, inner - 1):
-            tiles = list(own_term(tiles, level))
+        for level in range(1, inner):
+            if stream == 0:
+                load_node(level)
+            if level < inner - 1:
+                tiles = list(own_term(tiles, level))
         for group, tile in enumerate(own_term(tiles, inner - 1)):
             parts[stream][group][0][...] = tile.reshape(parts[stream][group][0].shape)
             send_part(stream, group, 0)

time: 27.2 us -> 27.5 us (1.011)
  Pallas kernels: 25.6 us -> 25.9 us
    pallas_call x1, Pallas kernels: 25.6 us -> 25.9 us  [per_device(): pl.pallas_call(functools.partial(kernel, n_leaf, n_grp), out_shape=jax.Sh...]
where the time goes in v8:
time: 27.5 us; the launch traced here: 27.3 us
  Pallas kernels  25.9 us (94%)
  local copies, waits for them, and re-layouts  1.32 us (5%)
    pallas_call x1, Pallas kernels, per_device(): pl.pallas_call(functools.partial(kernel, n_leaf, n_grp), out_shape=jax.Sh...  25.9 us
    unnamed x1, local copies, waits for them, and re-layouts  1.32 us

profile of v8, /device:TPU:0, one launch (start us, length us, event | category | flops | bytes accessed | tf_op | source)
XLA Modules:
  0.0 27.3 jit_solution(4960359012690213990)
XLA Ops:
  0.0 25.9 %shard_map.73 = bf16[16,512]{1,0:T(8,128)(2,1)} custom-call(bf16[1024,512]{1,0:T(8,128)(2,1)} %refs_0_.1, bf16[1024,512]{1,0:T(8,128)(2,1)} %refs_1_.1, bf16[1,512,512]{2,1,0:T(8,128)(2,1)} %refs_2_.1, bf16[1,1,3,1024,512]{4,3,2,1,0:T(8,128)(2,1)} %refs_3_.1, bf16[1,1,3,512,512]{4,3,2,1,0:T(8,128)(2,1)} %refs_4_.1, bf16[1,1,2,1024,512]{4,3,2,1,0:T(8,128)(2,1)} %refs_5_.1, ...), custom_call_target="tpu_custom_call" | custom-call | flops 8053063680 | bytes 10485760 | tf_op jit(solution)/shard_map/pallas_call | solution.py:269
  25.9 1.3 %copy.9 = bf16[512,16]{0,1:T(8,128)(2,1)} copy(bf16[512,16]{0,1:T(8,128)(2,1)} %bitcast.1) | data formatting | bytes 32768

commit v9 on v6

--- a/solution.py
+++ b/solution.py
@@ -131,28 +131,34 @@
     def half_basis(level, parity, span=slice(None)):
         return node_v[level, pl.ds(pl.multiple_of(parity * k, k), k), span]
 
-    rows = lax.broadcasted_iota(jnp.int32, (panel, panel), 0)
-    order = jnp.where(rows == target, 1.0, 0.0).astype(BF16)
+    mid = k // 2
+    spans = (slice(0, mid), slice(mid, k))
+
+    def leaf_order(start):
+        rows = lax.broadcasted_iota(jnp.int32, (half, panel), 0) + start
+        return jnp.where(rows == target, 1.0, 0.0).astype(BF16)
+
+    def leaf_tiles(turned, projected):
+        mixing = mix([projected[:, span] for span in spans], leaf_f)
+        for span in spans:
+            yield turned[:, span].astype(F32) - fold(dot_nt(mixing, leaf_v[span, :]))
+
+    order = leaf_order(half)
     loads[0].wait()
     turned = dot_nt(order, panel_v[...]).astype(BF16)
     loads[1].wait()
     loads[2].wait()
     for load in loads[3:]:
         load.start()
-    projected = dot(turned, leaf_v[...])
-
-    mid = k // 2
-    spans = (slice(0, mid), slice(mid, k))
-
-    def leaf_summit(ref, rows):
-        mixing = mix([projected[rows, span] for span in spans], leaf_f)
-        for span in spans:
-            ref[:, span] = turned[rows, span].astype(F32) - fold(dot_nt(mixing, leaf_v[span, :]))
-
-    leaf_summit(first, slice(half, panel))
-    pl.semaphore_wait(barrier, inner + n_grp - 1)
-    arriving = send(first, first_in, {"leaf": flipped(leaf, 1)})
-    leaf_summit(kept, slice(0, half))
+    arriving = []
+    for group, tile in enumerate(leaf_tiles(turned, dot(turned, leaf_v[...]))):
+        first[group] = tile
+        if group == 0:
+            pl.semaphore_wait(barrier, inner + n_grp - 1)
+        arriving.append(send(first.at[group], first_in.at[group], {"leaf": flipped(leaf, 1)}))
+    turned = dot_nt(leaf_order(0), panel_v[...]).astype(BF16)
+    for group, tile in enumerate(leaf_tiles(turned, dot(turned, leaf_v[...]))):
+        kept[group] = tile
 
     def project(stacked, level, parity):
         return [fold(dot(stacked, half_basis(level, parity, span))) for span in spans]
@@ -180,13 +186,14 @@
     for level in range(inner):
         load_node(level)
     parity = bit_of(leaf, 0)
-    own = project(stack(kept[...]), 0, parity)
-    arriving.wait_recv()
-    other = project(stack(first_in[...]), 0, 1 - parity)
+    own = project(join([stack(kept[group]) for group in range(2)]), 0, parity)
+    for copy in arriving:
+        copy.wait_recv()
+    other = project(join([stack(first_in[group]) for group in range(2)]), 0, 1 - parity)
     mixing = mix([left_tile + right_tile for left_tile, right_tile in zip(own, other)], node_f.at[0])
     summit = [
-        jnp.where(parity == 0, kept[:, span], first_in[:, span]) - fold(dot_nt(mixing, node_v[0, span, :]))
-        for span in spans]
+        jnp.where(parity == 0, kept[group], first_in[group]) - fold(dot_nt(mixing, node_v[0, span, :]))
+        for group, span in enumerate(spans)]
     for stream in streams:
         tiles = [tile[stream * stream_rows:(stream + 1) * stream_rows] for tile in summit]
         for level in range(1, inner - 1):
@@ -265,7 +272,7 @@
     steps = range(inner - 1)
     parts = [[[pltpu.VMEM(lead(inner - 1 - s), F32) for s in steps] for _ in range(2)] for _ in range(STREAMS)]
     parts_in = [[[pltpu.VMEM(lead(inner - 2 - s), F32) for s in steps] for _ in range(2)] for _ in range(STREAMS)]
-    copies = 1 + STREAMS * (2 * (inner - 1) + n_grp - 1)
+    copies = 2 + STREAMS * (2 * (inner - 1) + n_grp - 1)
     result = pl.pallas_call(
         functools.partial(kernel, n_leaf, n_grp),
         out_shape=jax.ShapeDtypeStruct((STREAMS * rows, k), BF16),
@@ -279,9 +286,9 @@
             pltpu.VMEM((levels,) + inner_tri.shape[-2:], BF16),
             pltpu.VMEM((outer, k, k), BF16),
             pltpu.VMEM((outer, k, k), BF16),
-            pltpu.VMEM((half, k), F32),
-            pltpu.VMEM((half, k), F32),
-            pltpu.VMEM((half, k), F32),
+            pltpu.VMEM((2, half, k // 2), F32),
+            pltpu.VMEM((2, half, k // 2), F32),
+            pltpu.VMEM((2, half, k // 2), F32),
             parts,
             parts_in,
             pltpu.VMEM((STREAMS, n_grp if scatter else 1, rows, k), F32),

time: 27.2 us -> 27.2 us (level)
  no operation moved by 1% of the time
where the time goes in v9:
time: 27.2 us; the launch traced here: 27 us
  Pallas kernels  25.7 us (94%)
  local copies, waits for them, and re-layouts  1.32 us (5%)
    pallas_call x1, Pallas kernels, per_device(): pl.pallas_call(functools.partial(kernel, n_leaf, n_grp), out_shape=jax.Sh...  25.7 us
    unnamed x1, local copies, waits for them, and re-layouts  1.32 us

profile of v9, /device:TPU:0, one launch (start us, length us, event | category | flops | bytes accessed | tf_op | source)
XLA Modules:
  0.0 27.0 jit_solution(17692444458622711959)
XLA Ops:
  0.0 25.7 %shard_map.73 = bf16[16,512]{1,0:T(8,128)(2,1)} custom-call(bf16[1024,512]{1,0:T(8,128)(2,1)} %refs_0_.1, bf16[1024,512]{1,0:T(8,128)(2,1)} %refs_1_.1, bf16[1,512,512]{2,1,0:T(8,128)(2,1)} %refs_2_.1, bf16[1,1,3,1024,512]{4,3,2,1,0:T(8,128)(2,1)} %refs_3_.1, bf16[1,1,3,512,512]{4,3,2,1,0:T(8,128)(2,1)} %refs_4_.1, bf16[1,1,2,1024,512]{4,3,2,1,0:T(8,128)(2,1)} %refs_5_.1, ...), custom_call_target="tpu_custom_call" | custom-call | flops 8053063680 | bytes 10485760 | tf_op jit(solution)/shard_map/pallas_call | solution.py:276
  25.7 1.3 %copy.9 = bf16[512,16]{0,1:T(8,128)(2,1)} copy(bf16[512,16]{0,1:T(8,128)(2,1)} %bitcast.1) | data formatting | bytes 32768
